TPU v7x, 32 devices: a whole 2x2x4 slice. The times are simulated.
32 devices in a mesh: tm: 2 (over y), space: 16 (over z, x, core).
Axes of the slice: x: 2, y: 2, z: 4, core: 2. Of those that a mesh axis runs over, the one named last changes fastest.
Arguments:
- frames_in: bfloat16 [4, 64, 128, 256], P('tm', 'space'), may hold values from -6 to 6
- w_space: bfloat16 [9, 256, 256], replicated, may hold values from -0.125 to 0.125
- w_time: bfloat16 [3, 256, 256], replicated, may hold values from -0.21875 to 0.21875
- grad_out: bfloat16 [4, 64, 128, 256], P('tm', 'space'), may hold values from -6 to 6
Outputs:
- block_out: bfloat16 [4, 64, 128, 256], P('tm', 'space')
- grad_in: bfloat16 [4, 64, 128, 256], P('tm', 'space')
- grad_space: float32 [9, 256, 256], P(None, 'tm', 'space')
- grad_time: float32 [3, 256, 256], P(None, 'tm', 'space')
All inputs are finite; a program needn't handle non-finite values.
Results may differ from a plain program's by a relative error of at most 0.0057.
Values may be sent and summed in bfloat16 or wider, within the bound.
A program may use at most 64 MiB of HBM per device.

v0:
```python
import jax
import jax.numpy as jnp
from jax import lax
from jax.sharding import PartitionSpec as P


def extended_2(block, sides, width):
    for axis, dim in sides:
        count = lax.axis_size(axis)
        forward = [(i, i + 1) for i in range(count - 1)]
        backward = [(target, source) for source, target in forward]
        low = lax.ppermute(
            lax.slice_in_dim(block, block.shape[dim] - width, None, axis=dim), axis, forward
        )
        high = lax.ppermute(lax.slice_in_dim(block, 0, width, axis=dim), axis, backward)
        block = jnp.concatenate([low, block, high], axis=dim)
    return block


def pad_columns(field):
    return jnp.pad(field, ((0, 0), (0, 0), (1, 1), (0, 0)))


def temporal(past_ext, grad_ext, w_time, count):
    chans = past_ext.shape[-1]
    shape = grad_ext[0:count].shape
    flat_grad = grad_ext[0:count].reshape(-1, chans)
    out_sum = jnp.zeros(flat_grad.shape, jnp.float32)
    back_sum = jnp.zeros(flat_grad.shape, jnp.float32)
    filters = []
    for k in range(3):
        source = past_ext[k : k + count].reshape(-1, chans)
        out_sum = out_sum + jnp.dot(source, w_time[k], preferred_element_type=jnp.float32)
        later = grad_ext[2 - k : 2 - k + count].reshape(-1, chans)
        back_sum = back_sum + lax.dot_general(
            later, w_time[k], (((1,), (1,)), ((), ())), preferred_element_type=jnp.float32
        )
        filters.append(
            lax.dot_general(
                flat_grad, source, (((0,), (0,)), ((), ())), preferred_element_type=jnp.float32
            )
        )
    return (
        out_sum.reshape(shape).astype(jnp.bfloat16),
        back_sum.reshape(shape).astype(jnp.bfloat16),
        jnp.stack(filters, axis=1),
    )


def body(frames_in, w_space, w_time, grad_out):
    count, height, width, chans = frames_in.shape
    extended = pad_columns(extended_2(frames_in, (("space", 1),), 1))
    pre = jnp.zeros((count * height * width, chans), jnp.float32)
    for i in range(3):
        for j in range(3):
            window = extended[:, i : i + height, j : j + width].reshape(-1, chans)
            pre = pre + jnp.dot(window, w_space[3 * i + j], preferred_element_type=jnp.float32)
    pre = pre.reshape(count, height, width, chans)
    hidden = jax.nn.silu(pre).astype(jnp.bfloat16)
    hid_cols, grad_cols = (
        lax.all_to_all(hidden, "tm", split_axis=2, concat_axis=0, tiled=True),
        lax.all_to_all(grad_out, "tm", split_axis=2, concat_axis=0, tiled=True),
    )
    blank = jnp.zeros((2,) + hid_cols.shape[1:], jnp.bfloat16)
    past_ext = jnp.concatenate([blank, hid_cols], axis=0)
    grad_ext = jnp.concatenate([grad_cols, blank], axis=0)
    out_cols, back_cols, time_terms = temporal(past_ext, grad_ext, w_time, hid_cols.shape[0])
    block_out, grad_hidden = (
        lax.all_to_all(out_cols, "tm", split_axis=0, concat_axis=2, tiled=True),
        lax.all_to_all(back_cols, "tm", split_axis=0, concat_axis=2, tiled=True),
    )
    sig = jax.nn.sigmoid(pre)
    grad_pre = (grad_hidden.astype(jnp.float32) * sig * (1.0 + pre * (1.0 - sig))).astype(
        jnp.bfloat16
    )
    grad_ext_rows = pad_columns(extended_2(grad_pre, (("space", 1),), 1))
    flat_pre = grad_pre.reshape(-1, chans)
    back = jnp.zeros((count * height * width, chans), jnp.float32)
    space_terms = []
    for i in range(3):
        for j in range(3):
            window = grad_ext_rows[:, 2 - i : 2 - i + height, 2 - j : 2 - j + width].reshape(
                -1, chans
            )
            back = back + lax.dot_general(
                window,
                w_space[3 * i + j],
                (((1,), (1,)), ((), ())),
                preferred_element_type=jnp.float32,
            )
            source = extended[:, i : i + height, j : j + width].reshape(-1, chans)
            space_terms.append(
                lax.dot_general(
                    flat_pre, source, (((0,), (0,)), ((), ())), preferred_element_type=jnp.float32
                )
            )
    grad_in = back.reshape(count, height, width, chans).astype(jnp.bfloat16)
    space_sum = jnp.stack(space_terms, axis=1)
    partial_space, partial_time = (
        lax.psum_scatter(space_sum, "space", scatter_dimension=0, tiled=True),
        lax.psum_scatter(time_terms, "space", scatter_dimension=0, tiled=True),
    )
    owned_space, owned_time = (
        lax.psum_scatter(partial_space, "tm", scatter_dimension=2, tiled=True),
        lax.psum_scatter(partial_time, "tm", scatter_dimension=2, tiled=True),
    )
    grad_space = jnp.transpose(owned_space, (1, 2, 0))
    grad_time = jnp.transpose(owned_time, (1, 2, 0))
    return (block_out, grad_in, grad_space, grad_time)


def solution(mesh):
    in_specs = (P("tm", "space", None, None), P(), P(), P("tm", "space", None, None))
    out_specs = (
        P("tm", "space", None, None),
        P("tm", "space", None, None),
        P(None, "tm", "space"),
        P(None, "tm", "space"),
    )
    return jax.shard_map(body, mesh=mesh, in_specs=in_specs, out_specs=out_specs, check_vma=False)
```

profile of v0, /device:TPU:0, one launch (start us, length us, event | category | flops | bytes accessed | tf_op | source)
XLA Modules:
  0.0 266.1 jit_solution(15114270632761067660)
XLA Ops:
  8.2 2.4 collective-permute-start
  10.6 1.3 collective-permute-start.1
  11.9 2.2 copy.53
  14.2 3.6 %all-to-all-start.2 = ((bf16[2,4,128,256]{3,1,0,2:T(4,128)(2,1)}), bf16[2,4,128,256]{3,1,0,2:T(4,128)(2,1)S(1)}, u32[]{:S(2)}, u32[]{:S(2)}) async-start(bf16[2,4,128,256]{3,1,0,2:T(4,128)(2,1)} %copy.53), calls=%async_computation.2 | async-start | bytes 1048576 | tf_op jit(solution)/shard_map/all_to_all | solution.py:62
  19.3 1.2 fusion.85
  23.4 1.3 convolution_add_fusion.12
  26.2 1.2 copy.55
  29.3 4.2 %all-to-all-start.3 = ((bf16[4,4,64,256]{3,2,1,0:T(8,128)(2,1)}), bf16[4,4,64,256]{3,2,1,0:T(8,128)(2,1)}, u32[]{:S(2)}, u32[]{:S(2)}) async-start(bf16[4,4,64,256]{3,2,1,0:T(8,128)(2,1)} %bitcast.272), calls=%async_computation.3 | async-start | bytes 1048576 | tf_op jit(solution)/shard_map/all_to_all | solution.py:70
  33.5 2.3 fusion.32
  35.8 5.6 %all-to-all-done.3 = bf16[4,4,64,256]{3,2,1,0:T(8,128)(2,1)} async-done(((bf16[4,4,64,256]{3,2,1,0:T(8,128)(2,1)}), bf16[4,4,64,256]{3,2,1,0:T(8,128)(2,1)}, u32[]{:S(2)}, u32[]{:S(2)}) %all-to-all-start.3) | async-done | bytes 524320 | tf_op jit(solution)/shard_map/all_to_all | solution.py:70
  41.5 1.3 convert_bitcast_fusion
  43.3 1.4 fusion.16
  46.9 1.2 copy.49
  48.1 4.2 %all-to-all-start = ((bf16[2,4,128,256]{3,1,0,2:T(4,128)(2,1)}), bf16[2,4,128,256]{3,1,0,2:T(4,128)(2,1)}, u32[]{:S(2)}, u32[]{:S(2)}) async-start(bf16[2,4,128,256]{3,1,0,2:T(4,128)(2,1)} %copy.49), calls=%async_computation | async-start | bytes 1048576 | tf_op jit(solution)/shard_map/all_to_all | solution.py:61
  52.4 3.9 %collective-permute-start.2 = (bf16[2,1,128,256]{3,2,1,0:T(8,128)(2,1)}, bf16[2,1,128,256]{3,2,1,0:T(8,128)(2,1)}, u32[]{:S(2)}, u32[]{:S(2)}) collective-permute-start(bf16[2,1,128,256]{3,2,1,0:T(8,128)(2,1)} %get-tuple-element.36), channel_id=1, source_target_pairs={{0,1},{1,2},{2,3},{3,4},{4,5},{5,6},{6,7},{7,8},{8,9},{9,10},{10,1... | collective-permute-start | bytes 393224 | tf_op jit(solution)/shard_map/ppermute | solution.py:12
  56.3 1.3 collective-permute-start.3
  63.8 1.4 convolution_bitcast_fusion
  68.1 2.5 copy.67
  74.1 1.2 select_maximum_fusion
  76.9 1.3 fusion.30
  80.6 1.3 convolution_add_fusion.1
  82.2 1.3 convolution_add_fusion.10
  83.5 85.4 %all-reduce.7.cloned.1.call-done = f32[256,3,256]{2,1,0:T(4,128)} async-done(((f32[256,3,256]{2,1,0:T(4,128)}), f32[256,3,256]{2,1,0:T(4,128)}) %all-reduce.7.cloned.1.call-update) | async-done | bytes 786448
  169.7 1.2 copy.92
  171.0 1.6 reshape.147
  172.6 2.5 fusion.4
  175.1 3.5 %all-to-all-start.1 = ((bf16[4,4,64,256]{3,2,1,0:T(8,128)(2,1)}), bf16[4,4,64,256]{3,2,1,0:T(8,128)(2,1)S(1)}, u32[]{:S(2)}, u32[]{:S(2)}) async-start(bf16[4,4,64,256]{3,2,1,0:T(8,128)(2,1)} %bitcast.271), calls=%async_computation.1 | async-start | bytes 1048576 | tf_op jit(solution)/shard_map/all_to_all | solution.py:69
  178.7 56.1 %reduce-scatter.6.cloned.1.call-done = f32[16,9,256]{2,0,1:T(8,128)} async-done(((f32[256,9,256]{2,0,1:T(8,128)}), f32[16,9,256]{2,0,1:T(8,128)}) %reduce-scatter.6.cloned.1.call-update) | async-done | bytes 147472 | tf_op jit(solution)/shard_map/reduce_scatter | solution.py:100
  234.8 2.0 fusion.3
  237.7 8.7 %reduce-scatter.10.cloned.1.call-done = f32[128,48]{1,0:T(8,128)} async-done(((f32[256,48]{1,0:T(8,128)}), f32[128,48]{1,0:T(8,128)}) %reduce-scatter.10.cloned.1.call-update) | async-done | bytes 24592
  246.4 1.4 reshape.148
  248.9 10.7 %reduce-scatter.8.cloned.1.call-done = f32[16,9,128]{2,0,1:T(8,128)} async-done(((f32[16,9,256]{2,0,1:T(8,128)}), f32[16,9,128]{2,0,1:T(8,128)}) %reduce-scatter.8.cloned.1.call-update) | async-done | bytes 73744 | tf_op jit(solution)/shard_map/reduce_scatter | solution.py:104
  (93 shorter events, 30.4 us)
Async XLA Ops:
  7.2 10.6 %copy-start.16 = (u32[32]{0:T(128)S(1)}, u32[32]{0:T(128)}, u32[]{:S(2)}) copy-start(u32[32]{0:T(128)} %constant.20) | copy-start | bytes 388
  7.2 11.9 %copy-start = (bf16[2,4,128,256]{3,2,1,0:T(8,128)(2,1)S(1)}, bf16[2,4,128,256]{3,2,1,0:T(8,128)(2,1)}, u32[]{:S(2)}) copy-start(bf16[2,4,128,256]{3,2,1,0:T(8,128)(2,1)} %param.4) | copy-start | bytes 1572868
  8.2 10.8 %collective-permute-start = (bf16[2,1,128,256]{3,2,1,0:T(8,128)(2,1)S(1)}, bf16[2,1,128,256]{3,2,1,0:T(8,128)(2,1)S(1)}, u32[]{:S(2)}, u32[]{:S(2)}) collective-permute-start(bf16[2,1,128,256]{3,2,1,0:T(8,128)(2,1)S(1)} %get-tuple-element.44), channel_id=1, source_target_pairs={{0,1},{1,2},{2,3},{3,4},{4,5},{5,6},{6,7},{7,8},{8,9},{9,10},{10,1... | collective-permute-start | bytes 393224 | tf_op jit(solution)/shard_map/ppermute | solution.py:12
  10.6 8.4 %collective-permute-start.1 = (bf16[2,1,128,256]{3,2,1,0:T(8,128)(2,1)S(1)}, bf16[2,1,128,256]{3,2,1,0:T(8,128)(2,1)S(1)}, u32[]{:S(2)}, u32[]{:S(2)}) collective-permute-start(bf16[2,1,128,256]{3,2,1,0:T(8,128)(2,1)S(1)} %get-tuple-element.45), channel_id=1, source_target_pairs={{1,0},{2,1},{3,2},{4,3},{5,4},{6,5},{7,6},{8,7},{9,8},{10,9},{11,1... | collective-permute-start | bytes 393224 | tf_op jit(solution)/shard_map/ppermute | solution.py:15
  14.2 11.2 %all-to-all-start.2 = ((bf16[2,4,128,256]{3,1,0,2:T(4,128)(2,1)}), bf16[2,4,128,256]{3,1,0,2:T(4,128)(2,1)S(1)}, u32[]{:S(2)}, u32[]{:S(2)}) async-start(bf16[2,4,128,256]{3,1,0,2:T(4,128)(2,1)} %copy.53), calls=%async_computation.2 | async-start | bytes 1048576 | tf_op jit(solution)/shard_map/all_to_all | solution.py:62
  19.3 1.3 copy-start.1
  21.7 0.8 copy-start.7
  25.4 0.8 copy-start.5
  26.1 1.3 copy-start.9
  29.3 12.2 %all-to-all-start.3 = ((bf16[4,4,64,256]{3,2,1,0:T(8,128)(2,1)}), bf16[4,4,64,256]{3,2,1,0:T(8,128)(2,1)}, u32[]{:S(2)}, u32[]{:S(2)}) async-start(bf16[4,4,64,256]{3,2,1,0:T(8,128)(2,1)} %bitcast.272), calls=%async_computation.3 | async-start | bytes 1048576 | tf_op jit(solution)/shard_map/all_to_all | solution.py:70
  41.5 1.4 copy-start.11
  41.5 1.7 copy-start.12
  41.5 1.8 copy-start.13
  45.9 11.7 %copy-start.8 = (bf16[2,4,128,256]{3,2,1,0:T(8,128)(2,1)S(1)}, bf16[2,4,128,256]{3,2,1,0:T(8,128)(2,1)}, u32[]{:S(2)}) copy-start(bf16[2,4,128,256]{3,2,1,0:T(8,128)(2,1)} %copy-done.7) | copy-start | bytes 1572868
  48.1 15.7 %all-to-all-start = ((bf16[2,4,128,256]{3,1,0,2:T(4,128)(2,1)}), bf16[2,4,128,256]{3,1,0,2:T(4,128)(2,1)}, u32[]{:S(2)}, u32[]{:S(2)}) async-start(bf16[2,4,128,256]{3,1,0,2:T(4,128)(2,1)} %copy.49), calls=%async_computation | async-start | bytes 1048576 | tf_op jit(solution)/shard_map/all_to_all | solution.py:61
  52.3 116.6 %all-reduce.7.cloned.1.call-start = ((), (), s32[]{:S(2)}) async-start(), calls=%async_computation.10 | async-start | bytes 2097152
  52.4 20.7 %collective-permute-start.2 = (bf16[2,1,128,256]{3,2,1,0:T(8,128)(2,1)}, bf16[2,1,128,256]{3,2,1,0:T(8,128)(2,1)}, u32[]{:S(2)}, u32[]{:S(2)}) collective-permute-start(bf16[2,1,128,256]{3,2,1,0:T(8,128)(2,1)} %get-tuple-element.36), channel_id=1, source_target_pairs={{0,1},{1,2},{2,3},{3,4},{4,5},{5,6},{6,7},{7,8},{8,9},{9,10},{10,1... | collective-permute-start | bytes 393224 | tf_op jit(solution)/shard_map/ppermute | solution.py:12
  56.3 16.8 %collective-permute-start.3 = (bf16[2,1,128,256]{3,2,1,0:T(8,128)(2,1)}, bf16[2,1,128,256]{3,2,1,0:T(8,128)(2,1)}, u32[]{:S(2)}, u32[]{:S(2)}) collective-permute-start(bf16[2,1,128,256]{3,2,1,0:T(8,128)(2,1)} %get-tuple-element.37), channel_id=1, source_target_pairs={{1,0},{2,1},{3,2},{4,3},{5,4},{6,5},{7,6},{8,7},{9,8},{10,9},{11,1... | collective-permute-start | bytes 393224 | tf_op jit(solution)/shard_map/ppermute | solution.py:15
  61.7 2.1 copy-start.6
  68.1 2.6 copy-start.14
  70.6 164.2 %reduce-scatter.6.cloned.1.call-start = ((), (), s32[]{:S(2)}) async-start(), calls=%async_computation.7 | async-start | bytes 2506752 | tf_op jit(solution)/shard_map/reduce_scatter | solution.py:100
  72.8 173.6 %reduce-scatter.10.cloned.1.call-start = ((), (), s32[]{:S(2)}) async-start(), calls=%async_computation.9 | async-start | bytes 196608
  75.3 1.3 copy-start.2
  78.9 1.0 copy-start.15
  80.6 1.3 copy-start.10
  172.6 62.2 %copy-start.3 = (f32[1024,256]{1,0:T(8,128)S(1)}, f32[1024,256]{1,0:T(8,128)}, u32[]{:S(2)}) copy-start(f32[1024,256]{1,0:T(8,128)} %convolution_add_fusion.1) | copy-start | bytes 3145732
  172.6 62.2 %copy-start.4 = (f32[1024,256]{1,0:T(8,128)S(1)}, f32[1024,256]{1,0:T(8,128)}, u32[]{:S(2)}) copy-start(f32[1024,256]{1,0:T(8,128)} %fusion.30) | copy-start | bytes 3145732
  175.1 61.7 %all-to-all-start.1 = ((bf16[4,4,64,256]{3,2,1,0:T(8,128)(2,1)}), bf16[4,4,64,256]{3,2,1,0:T(8,128)(2,1)S(1)}, u32[]{:S(2)}, u32[]{:S(2)}) async-start(bf16[4,4,64,256]{3,2,1,0:T(8,128)(2,1)} %bitcast.271), calls=%async_computation.1 | async-start | bytes 1048576 | tf_op jit(solution)/shard_map/all_to_all | solution.py:69
  178.6 81.0 %reduce-scatter.8.cloned.1.call-start = ((), (), s32[]{:S(2)}) async-start(), calls=%async_computation.8 | async-start | bytes 221184 | tf_op jit(solution)/shard_map/reduce_scatter | solution.py:104
Sparse Core Ops, SparseCore 0:
  70.7 98.0 all-reduce.6
  172.6 62.1 reduce-scatter.5
  237.1 9.2 reduce-scatter.9
  249.1 10.4 reduce-scatter.7
where the time goes:
time: 267 us; the launch traced here: 266 us
  waiting for transfers between devices  167 us (63%)
  matrix products  30.7 us (11%)
  starting transfers between devices  24.7 us (9%)
  local copies, waits for them, and re-layouts  22.6 us (8%)
  between operations  14.8 us (6%)
  other arithmetic  5.98 us (2%)
    unnamed x6, waiting for transfers between devices  94.2 us
    reduce_scatter x1, waiting for transfers between devices, body(): lax.psum_scatter(space_sum, 'space', scatter_dimension=0, tiled=True)  56.1 us
    unnamed x42, local copies, waits for them, and re-layouts  12 us
    reduce_scatter x1, waiting for transfers between devices, body(): lax.psum_scatter(partial_space, 'tm', scatter_dimension=2, tiled=True)  10.7 us
    dot_general x9, matrix products, body(): lax.dot_general(flat_pre, source, (((0,), (0,)), ((), ())), preferred_ele...  9.34 us
    dot_general x9, matrix products, body(): jnp.dot(window, w_space[3 * i + j], preferred_element_type=jnp.float32)  6.77 us
    dot_general x9, matrix products, body(): lax.dot_general(window, w_space[3 * i + j], (((1,), (1,)), ((), ())), pre...  6.62 us
    ppermute x2, starting transfers between devices, extended_2(): lax.ppermute(lax.slice_in_dim(block, block.shape[dim] - width, None, axis...  6.27 us
  transfers between devices with their start and end apart: 12, of which 6 were waited for; matrix products, arithmetic and copies ran while one was open for 17% of the time, Pallas kernels for 0%

commit v1 on v0

v1 whole, which is shorter than its diff:
```python
import jax
import jax.numpy as jnp
from jax import lax
from jax.sharding import PartitionSpec as P


def extended_2(block, sides, width):
    for axis, dim in sides:
        count = lax.axis_size(axis)
        forward = [(i, i + 1) for i in range(count - 1)]
        backward = [(target, source) for source, target in forward]
        low = lax.ppermute(
            lax.slice_in_dim(block, block.shape[dim] - width, None, axis=dim), axis, forward
        )
        high = lax.ppermute(lax.slice_in_dim(block, 0, width, axis=dim), axis, backward)
        block = jnp.concatenate([low, block, high], axis=dim)
    return block


def pad_columns(field):
    return jnp.pad(field, ((0, 0), (0, 0), (1, 1), (0, 0)))


def temporal_forward(past_ext, grad, w_time):
    count, chans = grad.shape[0], grad.shape[-1]
    flat_grad = grad.reshape(-1, chans)
    out_sum = jnp.zeros(flat_grad.shape, jnp.float32)
    filters = []
    for k in range(3):
        source = past_ext[k : k + count].reshape(-1, chans)
        out_sum = out_sum + jnp.dot(source, w_time[k], preferred_element_type=jnp.float32)
        filters.append(
            lax.dot_general(
                flat_grad, source, (((0,), (0,)), ((), ())), preferred_element_type=jnp.float32
            )
        )
    return out_sum.reshape(grad.shape).astype(jnp.bfloat16), filters


def temporal_backward(grad_ext, w_time, count):
    chans = grad_ext.shape[-1]
    back_sum = jnp.zeros((grad_ext[0:count].size // chans, chans), jnp.float32)
    for k in range(3):
        later = grad_ext[2 - k : 2 - k + count].reshape(-1, chans)
        back_sum = back_sum + lax.dot_general(
            later, w_time[k], (((1,), (1,)), ((), ())), preferred_element_type=jnp.float32
        )
    return back_sum.reshape(grad_ext[0:count].shape).astype(jnp.bfloat16)


def exchange(keep, send, axis, step):
    count = lax.axis_size(axis)
    got = lax.ppermute(send.astype(jnp.bfloat16), axis, [(i, i ^ step) for i in range(count)])
    return keep + got.astype(jnp.float32)


def halve_chunks(sums, axis, step):
    taps, chunks, rows, width = sums.shape
    pairs = sums.reshape(taps, chunks // 2, 2, rows, width)
    mine = lax.rem(lax.axis_index(axis) // step, 2)
    keep = lax.dynamic_index_in_dim(pairs, mine, 2, keepdims=False)
    send = lax.dynamic_index_in_dim(pairs, 1 - mine, 2, keepdims=False)
    return exchange(keep, send, axis, step)


def halve_width(sums, axis, step):
    half = sums.shape[3] // 2
    mine = lax.rem(lax.axis_index(axis) // step, 2)
    low, high = sums[..., :half], sums[..., half:]
    keep = jnp.where(mine == 0, low, high)
    send = jnp.where(mine == 0, high, low)
    return exchange(keep, send, axis, step)


def scatter_sums(sums):
    bands, groups = lax.axis_size("space"), lax.axis_size("tm")
    taps, rows, width = sums.shape
    sums = sums.reshape(taps, bands, rows // bands, width)
    sums = halve_chunks(sums, "space", 1)
    step = groups // 2
    while step >= 1:
        sums = halve_width(sums, "tm", step)
        step //= 2
    step = 2
    while step < bands:
        sums = halve_chunks(sums, "space", step)
        step *= 2
    return jnp.transpose(sums[:, 0], (0, 2, 1))


def body(frames_in, w_space, w_time, grad_out):
    count, height, width, chans = frames_in.shape
    groups = lax.axis_size("tm")
    onward = [(i, i + 1) for i in range(groups - 1)]
    grad_next = lax.ppermute(grad_out[:2], "tm", [(t, s) for s, t in onward])
    extended = pad_columns(extended_2(frames_in, (("space", 1),), 1))
    pre = jnp.zeros((count * height * width, chans), jnp.float32)
    for i in range(3):
        for j in range(3):
            window = extended[:, i : i + height, j : j + width].reshape(-1, chans)
            pre = pre + jnp.dot(window, w_space[3 * i + j], preferred_element_type=jnp.float32)
    pre = pre.reshape(count, height, width, chans)
    hidden = jax.nn.silu(pre).astype(jnp.bfloat16)
    past = lax.ppermute(hidden[count - 2 :], "tm", onward)
    grad_hidden = temporal_backward(
        jnp.concatenate([grad_out, grad_next], axis=0), w_time, count
    )
    sig = jax.nn.sigmoid(pre)
    grad_pre = (grad_hidden.astype(jnp.float32) * sig * (1.0 + pre * (1.0 - sig))).astype(
        jnp.bfloat16
    )
    grad_ext_rows = pad_columns(extended_2(grad_pre, (("space", 1),), 1))
    flat_pre = grad_pre.reshape(-1, chans)
    terms = []
    for i in range(3):
        for j in range(3):
            source = extended[:, i : i + height, j : j + width].reshape(-1, chans)
            terms.append(
                lax.dot_general(
                    flat_pre, source, (((0,), (0,)), ((), ())), preferred_element_type=jnp.float32
                )
            )
    block_out, time_terms = temporal_forward(
        jnp.concatenate([past, hidden], axis=0), grad_out, w_time
    )
    owned = scatter_sums(jnp.stack(terms + time_terms))
    back = jnp.zeros((count * height * width, chans), jnp.float32)
    for i in range(3):
        for j in range(3):
            window = grad_ext_rows[:, 2 - i : 2 - i + height, 2 - j : 2 - j + width].reshape(
                -1, chans
            )
            back = back + lax.dot_general(
                window,
                w_space[3 * i + j],
                (((1,), (1,)), ((), ())),
                preferred_element_type=jnp.float32,
            )
    grad_in = back.reshape(count, height, width, chans).astype(jnp.bfloat16)
    return (block_out, grad_in, owned[:9], owned[9:])


def solution(mesh):
    in_specs = (P("tm", "space", None, None), P(), P(), P("tm", "space", None, None))
    out_specs = (
        P("tm", "space", None, None),
        P("tm", "space", None, None),
        P(None, "tm", "space"),
        P(None, "tm", "space"),
    )
    return jax.shard_map(body, mesh=mesh, in_specs=in_specs, out_specs=out_specs, check_vma=False)
```

time: 267 us -> 80.3 us (0.30)
  waiting for transfers between devices: 167 us -> 23.6 us
  local copies, waits for them, and re-layouts: 22.6 us -> 8.61 us
  between operations: 14.8 us -> 1.27 us
  matrix products: 30.7 us -> 18.4 us
    unnamed x6 -> x0, waiting for transfers between devices: 94.2 us -> none
    reduce_scatter x2 -> x0, waiting for transfers between devices: 66.8 us -> none  [the longest x1 56.1 us: body(): lax.psum_scatter(space_sum, 'space', scatter_dimension=0, tiled=True)]
    ppermute x0 -> x7, waiting for transfers between devices: none -> 22.3 us  [the longest x5 18.4 us: exchange(): lax.ppermute(send.astype(jnp.bfloat16), axis, [(i, i ^ step) for i in ran...]
    all_to_all x4 -> x0, starting transfers between devices: 15.5 us -> none  [the longest x1 4.22 us: body(): lax.all_to_all(hidden, 'tm', split_axis=2, concat_axis=0, tiled=True)]
    ppermute x0 -> x7, starting transfers between devices: none -> 14.4 us  [the longest x5 11.5 us: exchange(): lax.ppermute(send.astype(jnp.bfloat16), axis, [(i, i ^ step) for i in ran...]
    unnamed x42 -> x34, local copies, waits for them, and re-layouts: 12 us -> 3.49 us
    all_to_all x4 -> x0, waiting for transfers between devices: 6.33 us -> none  [the longest x1 5.64 us: body(): lax.all_to_all(back_cols, 'tm', split_axis=0, concat_axis=2, tiled=True)]
    dot_general x9, matrix products: 9.34 us -> 5.14 us  [body(): lax.dot_general(flat_pre, source, (((0,), (0,)), ((), ())), preferred_ele...]
  transfers between devices with their start and end apart: 12 -> 11, of which waited for: 6 -> 7; matrix products, arithmetic and copies ran while one was open for 17% -> 27% of each run, Pallas kernels for 0% -> 0%
where the time goes in v1:
time: 80.3 us; the launch traced here: 79.7 us
  starting transfers between devices  24.2 us (30%)
  waiting for transfers between devices  23.6 us (29%)
  matrix products  18.4 us (23%)
  local copies, waits for them, and re-layouts  8.61 us (11%)
  other arithmetic  3.67 us (5%)
  between operations  1.27 us (2%)
    ppermute x5, waiting for transfers between devices, exchange(): lax.ppermute(send.astype(jnp.bfloat16), axis, [(i, i ^ step) for i in ran...  18.4 us
    ppermute x5, starting transfers between devices, exchange(): lax.ppermute(send.astype(jnp.bfloat16), axis, [(i, i ^ step) for i in ran...  11.5 us
    ppermute x2, starting transfers between devices, extended_2(): lax.ppermute(lax.slice_in_dim(block, block.shape[dim] - width, None, axis...  7.07 us
    dot_general x9, matrix products, body(): lax.dot_general(flat_pre, source, (((0,), (0,)), ((), ())), preferred_ele...  5.14 us
    dot_general x9, matrix products, body(): lax.dot_general(window, w_space[3 * i + j], (((1,), (1,)), ((), ())), pre...  4 us
    ppermute x1, waiting for transfers between devices, body(): grad_next = lax.ppermute(grad_out[:2], 'tm', [(t, s) for s, t in onward])  3.95 us
    unnamed x34, local copies, waits for them, and re-layouts  3.49 us
    dot_general x3, matrix products, temporal_forward(): jnp.dot(source, w_time[k], preferred_element_type=jnp.float32)  2.78 us
  transfers between devices with their start and end apart: 11, of which 7 were waited for; matrix products, arithmetic and copies ran while one was open for 27% of the time, Pallas kernels for 0%

profile of v1, /device:TPU:0, one launch (start us, length us, event | category | flops | bytes accessed | tf_op | source)
XLA Modules:
  0.0 79.7 jit_solution(3504802594699008598)
XLA Ops:
  0.6 1.0 %fusion.104 = (bf16[2,1,128,256]{3,2,1,0:T(8,128)(2,1)S(1)}, bf16[2,1,128,256]{3,2,1,0:T(8,128)(2,1)S(1)}) fusion(bf16[2,4,128,256]{3,2,1,0:T(8,128)(2,1)} %param.4), kind=kLoop, calls=%fused_computation.160 | loop fusion | bytes 524288 | tf_op jit(solution)/shard_map/slice | solution.py:13
  1.7 2.4 %collective-permute-start = (bf16[2,1,128,256]{3,2,1,0:T(8,128)(2,1)S(1)}, bf16[2,1,128,256]{3,2,1,0:T(8,128)(2,1)S(1)}, u32[]{:S(2)}, u32[]{:S(2)}) collective-permute-start(bf16[2,1,128,256]{3,2,1,0:T(8,128)(2,1)S(1)} %get-tuple-element.24), channel_id=1, source_target_pairs={{0,1},{1,2},{2,3},{3,4},{4,5},{5,6},{6,7},{7,8},{8,9},{9,10},{10,1... | collective-permute-start | bytes 393224 | tf_op jit(solution)/shard_map/ppermute | solution.py:12
  4.1 1.3 %collective-permute-start.1 = (bf16[2,1,128,256]{3,2,1,0:T(8,128)(2,1)S(1)}, bf16[2,1,128,256]{3,2,1,0:T(8,128)(2,1)S(1)}, u32[]{:S(2)}, u32[]{:S(2)}) collective-permute-start(bf16[2,1,128,256]{3,2,1,0:T(8,128)(2,1)S(1)} %get-tuple-element.25), channel_id=1, source_target_pairs={{1,0},{2,1},{3,2},{4,3},{5,4},{6,5},{7,6},{8,7},{9,8},{10,9},{11,1... | collective-permute-start | bytes 393224 | tf_op jit(solution)/shard_map/ppermute | solution.py:15
  5.4 1.3 %collective-permute-start.3 = (bf16[2,4,128,256]{3,2,1,0:T(8,128)(2,1)}, bf16[2,4,128,256]{3,2,1,0:T(8,128)(2,1)S(1)}, u32[]{:S(2)}, u32[]{:S(2)}) collective-permute-start(bf16[2,4,128,256]{3,2,1,0:T(8,128)(2,1)} %param.7), channel_id=1, source_target_pairs={{16,0},{17,1},{18,2},{19,3},{20,4},{21,5},{22,6},{23,7},{24,8},{25... | collective-permute-start | bytes 1572872 | tf_op jit(solution)/shard_map/ppermute | solution.py:95
  6.7 1.4 %fusion.36 = f32[1024,256]{1,0:T(8,128)S(1)} fusion(bf16[1024,256]{1,0:T(8,128)(2,1)} %bitcast.284, bf16[3,256,256]{2,1,0:T(8,128)(2,1)} %param.6), kind=kOutput, calls=%fused_computation.87 | convolution fusion | flops 134217728 | bytes 1703936 | tf_op jit(solution)/shard_map/dot_general | solution.py:45
  8.1 1.3 %collective-permute-done.1 = bf16[2,1,128,256]{3,2,1,0:T(8,128)(2,1)S(1)} collective-permute-done((bf16[2,1,128,256]{3,2,1,0:T(8,128)(2,1)S(1)}, bf16[2,1,128,256]{3,2,1,0:T(8,128)(2,1)S(1)}, u32[]{:S(2)}, u32[]{:S(2)}) %collective-permute-start.1) | collective-permute-done | bytes 131104 | tf_op jit(solution)/shard_map/ppermute | solution.py:15
  10.1 0.8 %copy-done.6 = bf16[9,256,256]{2,1,0:T(8,128)(2,1)S(1)} copy-done((bf16[9,256,256]{2,1,0:T(8,128)(2,1)S(1)}, bf16[9,256,256]{2,1,0:T(8,128)(2,1)}, u32[]{:S(2)}) %copy-start.6) | copy-done | bytes 1179672
  13.9 0.7 copy-done.12
  14.6 1.4 %fusion.34 = f32[1024,256]{1,0:T(8,128)} fusion(f32[1024,256]{1,0:T(8,128)S(1)} %fusion.4, bf16[3,256,256]{2,1,0:T(8,128)(2,1)S(1)} %copy-done.12), kind=kOutput, calls=%fused_computation.81 | convolution fusion | flops 135528448 | bytes 2228224 | tf_op jit(solution)/shard_map/dot_general | solution.py:31
  16.0 4.0 %collective-permute-done.3 = bf16[2,4,128,256]{3,2,1,0:T(8,128)(2,1)S(1)} collective-permute-done((bf16[2,4,128,256]{3,2,1,0:T(8,128)(2,1)}, bf16[2,4,128,256]{3,2,1,0:T(8,128)(2,1)S(1)}, u32[]{:S(2)}, u32[]{:S(2)}) %collective-permute-start.3) | collective-permute-done | bytes 524320 | tf_op jit(solution)/shard_map/ppermute | solution.py:95
  21.2 1.1 %fusion.106 = f32[256,256,1,1]{0,1,3,2:T(8,128)} fusion(bf16[2,4,128,256]{3,2,1,0:T(8,128)(2,1)S(1)} %get-tuple-element.5, bf16[2,4,128,256]{3,2,1,0:T(8,128)(2,1)S(1)} %copy-done), kind=kOutput, calls=%fused_computation.162 | convolution fusion | flops 134217728 | bytes 1310720 | tf_op jit(solution)/shard_map/dot_general | solution.py:33
  22.2 1.6 %collective-permute-start.2 = (bf16[2,4,128,256]{3,2,1,0:T(8,128)(2,1)S(1)}, bf16[2,4,128,256]{3,2,1,0:T(8,128)(2,1)S(1)}, u32[]{:S(2)}, u32[]{:S(2)}) collective-permute-start(bf16[2,4,128,256]{3,2,1,0:T(8,128)(2,1)S(1)} %get-tuple-element.5), channel_id=1, source_target_pairs={{0,16},{1,17},{2,18},{3,19},{4,20},{5,21},{6,22},{7,23},{8,24},{9,... | collective-permute-start | bytes 1572872 | tf_op jit(solution)/shard_map/ppermute | solution.py:104
  23.8 0.7 fusion.103
  24.6 4.7 %collective-permute-start.4 = (bf16[2,1,128,256]{3,2,1,0:T(8,128)(2,1)}, bf16[2,1,128,256]{3,2,1,0:T(8,128)(2,1)}, u32[]{:S(2)}, u32[]{:S(2)}) collective-permute-start(bf16[2,1,128,256]{3,2,1,0:T(8,128)(2,1)} %get-tuple-element.20), channel_id=1, source_target_pairs={{0,1},{1,2},{2,3},{3,4},{4,5},{5,6},{6,7},{7,8},{8,9},{9,10},{10,1... | collective-permute-start | bytes 393224 | tf_op jit(solution)/shard_map/ppermute | solution.py:12
  29.3 1.5 %collective-permute-start.5 = (bf16[2,1,128,256]{3,2,1,0:T(8,128)(2,1)}, bf16[2,1,128,256]{3,2,1,0:T(8,128)(2,1)}, u32[]{:S(2)}, u32[]{:S(2)}) collective-permute-start(bf16[2,1,128,256]{3,2,1,0:T(8,128)(2,1)} %get-tuple-element.21), channel_id=1, source_target_pairs={{1,0},{2,1},{3,2},{4,3},{5,4},{6,5},{7,6},{8,7},{9,8},{10,9},{11,1... | collective-permute-start | bytes 393224 | tf_op jit(solution)/shard_map/ppermute | solution.py:15
  30.7 1.0 %copy.20 = bf16[256,2,4,128]{3,0,2,1:T(8,128)(2,1)} copy(bf16[256,2,4,128]{0,3,2,1:T(8,128)(2,1)S(1)} %bitcast.286) | data formatting | bytes 1048576 | tf_op jit(solution)/shard_map/dot_general | solution.py:119
  31.7 1.4 %fusion.17 = f32[12,8,2,16,256]{4,3,2,1,0:T(8,128)S(1)} fusion(bf16[8,2,16,2,4,128]{5,2,1,0,4,3:T(8,128)(2,1)} %bitcast.288, bf16[2,6,130,256]{3,2,1,0:T(8,128)(2,1)S(1)} %select_maximum_fusion.2), kind=kOutput, calls=%fused_computation.46 | convolution fusion | flops 134217728 | bytes 1310720 | tf_op jit(solution)/shard_map/dot_general | solution.py:119
  33.2 1.5 %fusion.16 = f32[12,8,2,16,256]{4,3,2,1,0:T(8,128)S(1)} fusion(f32[12,8,2,16,256]{4,3,2,1,0:T(8,128)S(1)} %fusion.17, bf16[8,2,16,2,4,128]{5,2,1,0,4,3:T(8,128)(2,1)} %bitcast.289, bf16[2,4,128,256]{3,2,1,0:T(8,128)(2,1)} %copy-done.3), kind=kOutput, calls=%fused_computation.44 | convolution fusion | flops 134217728 | bytes 1310720 | tf_op jit(solution)/shard_map/dot_general | solution.py:119
  37.4 1.2 %select_maximum_fusion = bf16[2,6,130,256]{3,2,1,0:T(8,128)(2,1)S(1)} fusion(bf16[2,1,128,256]{3,2,1,0:T(8,128)(2,1)} %collective-permute-done.5, bf16[2,4,128,256]{3,2,1,0:T(8,128)(2,1)S(1)} %get-tuple-element.4, bf16[2,1,128,256]{3,2,1,0:T(8,128)(2,1)} %collective-permute-done.4), kind=kLoop, calls=%fused_computation.57 | loop fusion | flops 4792320 | bytes 1585152 | tf_op jit(solution)/shard_map/concatenate | solution.py:16
  39.0 0.8 %copy-done.7 = bf16[9,256,256]{2,1,0:T(8,128)(2,1)S(1)} copy-done((bf16[9,256,256]{2,1,0:T(8,128)(2,1)S(1)}, bf16[9,256,256]{2,1,0:T(8,128)(2,1)}, u32[]{:S(2)}) %copy-start.7) | copy-done | bytes 1179672
  40.1 1.1 %pad_maximum_fusion = (bf16[2,4,128,256]{3,2,1,0:T(8,128)(2,1)S(1)}, bf16[2,4,128,256]{3,2,1,0:T(8,128)(2,1)S(1)}) fusion(bf16[2,4,128,256]{3,2,1,0:T(8,128)(2,1)S(1)} %get-tuple-element.4, bf16[2,1,128,256]{3,2,1,0:T(8,128)(2,1)} %collective-permute-done.4, bf16[2,1,128,256]{3,2,1,0:T(8,128)(2,1)} %collective-permute-done.5), kind=kLoop, calls=%fused_computation.65 | loop fusion | flops 524288 | bytes 1835008 | tf_op jit(solution)/shard_map/concatenate | solution.py:16
  43.4 4.2 %collective-permute-start.6 = (bf16[12,8,16,256]{3,2,1,0:T(8,128)(2,1)S(1)}, bf16[12,8,16,256]{3,2,1,0:T(8,128)(2,1)S(1)}, u32[]{:S(2)}, u32[]{:S(2)}) collective-permute-start(bf16[12,8,16,256]{3,2,1,0:T(8,128)(2,1)S(1)} %fusion.23), channel_id=1, source_target_pairs={{0,1},{1,0},{2,3},{3,2},{4,5},{5,4},{6,7},{7,6},{8,9},{9,8},{10,11... | collective-permute-start | bytes 2359304 | tf_op jit(solution)/shard_map/ppermute | solution.py:53
  48.8 0.6 collective-permute-done.6
  50.5 10.8 %collective-permute-done.7 = bf16[12,8,16,128]{3,2,1,0:T(8,128)(2,1)S(1)} collective-permute-done((bf16[12,8,16,128]{3,2,1,0:T(8,128)(2,1)S(1)}, bf16[12,8,16,128]{3,2,1,0:T(8,128)(2,1)S(1)}, u32[]{:S(2)}, u32[]{:S(2)}) %collective-permute-start.7) | collective-permute-done | bytes 393248 | tf_op jit(solution)/shard_map/ppermute | solution.py:53
  61.5 1.7 %collective-permute-start.8 = (bf16[12,4,16,128]{3,2,1,0:T(8,128)(2,1)S(1)}, bf16[12,4,16,128]{3,2,1,0:T(8,128)(2,1)S(1)}, u32[]{:S(2)}, u32[]{:S(2)}) collective-permute-start(bf16[12,4,16,128]{3,2,1,0:T(8,128)(2,1)S(1)} %fusion.35), channel_id=1, source_target_pairs={{0,2},{1,3},{2,0},{3,1},{4,6},{5,7},{6,4},{7,5},{8,10},{9,11},{10,... | collective-permute-start | bytes 589832 | tf_op jit(solution)/shard_map/ppermute | solution.py:53
  63.2 1.1 %fusion.7 = bf16[1024,256]{1,0:T(8,128)(2,1)} fusion(f32[1024,256]{1,0:T(8,128)S(1)} %fusion.45, f32[1024,256]{1,0:T(8,128)S(1)} %convolution_add_fusion.1, bf16[1024,256]{1,0:T(8,128)(2,1)S(1)} %bitcast.303, bf16[9,256,256]{2,1,0:T(8,128)(2,1)S(1)} %copy-done.7), kind=kOutput, calls=%fused_computation.27 | convolution fusion | flops 135004160 | bytes 3276800 | tf_op jit(solution)/shard_map/dot_general | solution.py:133
  64.4 3.6 %collective-permute-done.8 = bf16[12,4,16,128]{3,2,1,0:T(8,128)(2,1)S(1)} collective-permute-done((bf16[12,4,16,128]{3,2,1,0:T(8,128)(2,1)S(1)}, bf16[12,4,16,128]{3,2,1,0:T(8,128)(2,1)S(1)}, u32[]{:S(2)}, u32[]{:S(2)}) %collective-permute-start.8) | collective-permute-done | bytes 196640 | tf_op jit(solution)/shard_map/ppermute | solution.py:53
  68.2 2.2 %collective-permute-start.9 = (bf16[12,2,16,128]{3,2,1,0:T(8,128)(2,1)S(1)}, bf16[12,2,16,128]{3,2,1,0:T(8,128)(2,1)S(1)}, u32[]{:S(2)}, u32[]{:S(2)}) collective-permute-start(bf16[12,2,16,128]{3,2,1,0:T(8,128)(2,1)S(1)} %fusion.91), channel_id=1, source_target_pairs={{0,4},{1,5},{2,6},{3,7},{4,0},{5,1},{6,2},{7,3},{8,12},{9,13},{10,... | collective-permute-start | bytes 294920 | tf_op jit(solution)/shard_map/ppermute | solution.py:53
  70.6 2.3 %collective-permute-done.9 = bf16[12,2,16,128]{3,2,1,0:T(8,128)(2,1)S(1)} collective-permute-done((bf16[12,2,16,128]{3,2,1,0:T(8,128)(2,1)S(1)}, bf16[12,2,16,128]{3,2,1,0:T(8,128)(2,1)S(1)}, u32[]{:S(2)}, u32[]{:S(2)}) %collective-permute-start.9) | collective-permute-done | bytes 98336 | tf_op jit(solution)/shard_map/ppermute | solution.py:53
  73.0 3.4 %collective-permute-start.10 = (bf16[12,1,16,128]{3,2,1,0:T(8,128)(2,1)S(1)}, bf16[12,1,16,128]{3,2,1,0:T(8,128)(2,1)S(1)}, u32[]{:S(2)}, u32[]{:S(2)}) collective-permute-start(bf16[12,1,16,128]{3,2,1,0:T(8,128)(2,1)S(1)} %dynamic-slice_convert_fusion.2), channel_id=1, source_target_pairs={{0,8},{1,9},{2,10},{3,11},{4,12},{5,13},{6,14},{7,15},{8,0},{9,1},... | collective-permute-start | bytes 147464 | tf_op jit(solution)/shard_map/ppermute | solution.py:53
  76.4 1.1 %fusion.5 = bf16[1024,256]{1,0:T(8,128)(2,1)} fusion(f32[1024,256]{1,0:T(8,128)S(1)} %copy-done.14, f32[1024,256]{1,0:T(8,128)S(1)} %fusion.41, bf16[1024,256]{1,0:T(8,128)(2,1)S(1)} %bitcast.287, bf16[3,256,256]{2,1,0:T(8,128)(2,1)S(1)} %copy-done.13), kind=kOutput, calls=%fused_computation.25 | convolution fusion | flops 135004160 | bytes 3276800 | tf_op jit(solution)/shard_map/dot_general | solution.py:31
  77.5 1.0 %collective-permute-done.10 = bf16[12,1,16,128]{3,2,1,0:T(8,128)(2,1)S(1)} collective-permute-done((bf16[12,1,16,128]{3,2,1,0:T(8,128)(2,1)S(1)}, bf16[12,1,16,128]{3,2,1,0:T(8,128)(2,1)S(1)}, u32[]{:S(2)}, u32[]{:S(2)}) %collective-permute-start.10) | collective-permute-done | bytes 49184 | tf_op jit(solution)/shard_map/ppermute | solution.py:53
  (85 shorter events, 14.4 us)
Async XLA Ops:
  0.6 8.8 %copy-start.1 = (bf16[2,4,128,256]{3,2,1,0:T(8,128)(2,1)S(1)}, bf16[2,4,128,256]{3,2,1,0:T(8,128)(2,1)}, u32[]{:S(2)}) copy-start(bf16[2,4,128,256]{3,2,1,0:T(8,128)(2,1)} %param.4) | copy-start | bytes 1572868
  1.7 6.4 %collective-permute-start = (bf16[2,1,128,256]{3,2,1,0:T(8,128)(2,1)S(1)}, bf16[2,1,128,256]{3,2,1,0:T(8,128)(2,1)S(1)}, u32[]{:S(2)}, u32[]{:S(2)}) collective-permute-start(bf16[2,1,128,256]{3,2,1,0:T(8,128)(2,1)S(1)} %get-tuple-element.24), channel_id=1, source_target_pairs={{0,1},{1,2},{2,3},{3,4},{4,5},{5,6},{6,7},{7,8},{8,9},{9,10},{10,1... | collective-permute-start | bytes 393224 | tf_op jit(solution)/shard_map/ppermute | solution.py:12
  4.1 5.3 %collective-permute-start.1 = (bf16[2,1,128,256]{3,2,1,0:T(8,128)(2,1)S(1)}, bf16[2,1,128,256]{3,2,1,0:T(8,128)(2,1)S(1)}, u32[]{:S(2)}, u32[]{:S(2)}) collective-permute-start(bf16[2,1,128,256]{3,2,1,0:T(8,128)(2,1)S(1)} %get-tuple-element.25), channel_id=1, source_target_pairs={{1,0},{2,1},{3,2},{4,3},{5,4},{6,5},{7,6},{8,7},{9,8},{10,9},{11,1... | collective-permute-start | bytes 393224 | tf_op jit(solution)/shard_map/ppermute | solution.py:15
  5.4 14.6 %collective-permute-start.3 = (bf16[2,4,128,256]{3,2,1,0:T(8,128)(2,1)}, bf16[2,4,128,256]{3,2,1,0:T(8,128)(2,1)S(1)}, u32[]{:S(2)}, u32[]{:S(2)}) collective-permute-start(bf16[2,4,128,256]{3,2,1,0:T(8,128)(2,1)} %param.7), channel_id=1, source_target_pairs={{16,0},{17,1},{18,2},{19,3},{20,4},{21,5},{22,6},{23,7},{24,8},{25... | collective-permute-start | bytes 1572872 | tf_op jit(solution)/shard_map/ppermute | solution.py:95
  9.6 1.3 %copy-start.6 = (bf16[9,256,256]{2,1,0:T(8,128)(2,1)S(1)}, bf16[9,256,256]{2,1,0:T(8,128)(2,1)}, u32[]{:S(2)}) copy-start(bf16[9,256,256]{2,1,0:T(8,128)(2,1)} %param.5) | copy-start | bytes 3538948
  11.6 0.8 copy-start.3
  11.6 2.0 %copy-start.4 = (bf16[2,4,128,256]{3,2,1,0:T(8,128)(2,1)}, bf16[2,4,128,256]{3,2,1,0:T(8,128)(2,1)S(1)}, u32[]{:S(2)}) copy-start(bf16[2,4,128,256]{3,2,1,0:T(8,128)(2,1)S(1)} %get-tuple-element.22) | copy-start | bytes 1572868
  13.6 1.0 %copy-start.12 = (bf16[3,256,256]{2,1,0:T(8,128)(2,1)S(1)}, bf16[3,256,256]{2,1,0:T(8,128)(2,1)}, u32[]{:S(2)}) copy-start(bf16[3,256,256]{2,1,0:T(8,128)(2,1)} %param.6) | copy-start | bytes 1179652
  14.6 6.1 %copy-start.8 = (f32[1024,256]{1,0:T(8,128)}, f32[1024,256]{1,0:T(8,128)S(1)}, u32[]{:S(2)}) copy-start(f32[1024,256]{1,0:T(8,128)S(1)} %fusion.4) | copy-start | bytes 3145732
  14.6 5.4 %copy-start = (bf16[2,4,128,256]{3,2,1,0:T(8,128)(2,1)S(1)}, bf16[2,4,128,256]{3,2,1,0:T(8,128)(2,1)}, u32[]{:S(2)}) copy-start(bf16[2,4,128,256]{3,2,1,0:T(8,128)(2,1)} %param.7) | copy-start | bytes 1572868
  20.7 1.6 %copy-start.10 = (f32[1024,256]{1,0:T(8,128)}, f32[1024,256]{1,0:T(8,128)S(1)}, u32[]{:S(2)}) copy-start(f32[1024,256]{1,0:T(8,128)S(1)} %fusion.8) | copy-start | bytes 3145732
  22.2 19.6 %collective-permute-start.2 = (bf16[2,4,128,256]{3,2,1,0:T(8,128)(2,1)S(1)}, bf16[2,4,128,256]{3,2,1,0:T(8,128)(2,1)S(1)}, u32[]{:S(2)}, u32[]{:S(2)}) collective-permute-start(bf16[2,4,128,256]{3,2,1,0:T(8,128)(2,1)S(1)} %get-tuple-element.5), channel_id=1, source_target_pairs={{0,16},{1,17},{2,18},{3,19},{4,20},{5,21},{6,22},{7,23},{8,24},{9,... | collective-permute-start | bytes 1572872 | tf_op jit(solution)/shard_map/ppermute | solution.py:104
  24.6 12.8 %collective-permute-start.4 = (bf16[2,1,128,256]{3,2,1,0:T(8,128)(2,1)}, bf16[2,1,128,256]{3,2,1,0:T(8,128)(2,1)}, u32[]{:S(2)}, u32[]{:S(2)}) collective-permute-start(bf16[2,1,128,256]{3,2,1,0:T(8,128)(2,1)} %get-tuple-element.20), channel_id=1, source_target_pairs={{0,1},{1,2},{2,3},{3,4},{4,5},{5,6},{6,7},{7,8},{8,9},{9,10},{10,1... | collective-permute-start | bytes 393224 | tf_op jit(solution)/shard_map/ppermute | solution.py:12
  29.3 8.1 %collective-permute-start.5 = (bf16[2,1,128,256]{3,2,1,0:T(8,128)(2,1)}, bf16[2,1,128,256]{3,2,1,0:T(8,128)(2,1)}, u32[]{:S(2)}, u32[]{:S(2)}) collective-permute-start(bf16[2,1,128,256]{3,2,1,0:T(8,128)(2,1)} %get-tuple-element.21), channel_id=1, source_target_pairs={{1,0},{2,1},{3,2},{4,3},{5,4},{6,5},{7,6},{8,7},{9,8},{10,9},{11,1... | collective-permute-start | bytes 393224 | tf_op jit(solution)/shard_map/ppermute | solution.py:15
  31.7 2.9 %copy-start.2 = (bf16[256,2,4,128]{3,0,2,1:T(8,128)(2,1)S(1)}, bf16[256,2,4,128]{3,0,2,1:T(8,128)(2,1)}, u32[]{:S(2)}) copy-start(bf16[256,2,4,128]{3,0,2,1:T(8,128)(2,1)} %copy.20) | copy-start | bytes 1572868
  35.6 1.0 %copy-start.5 = (bf16[2,4,128,256]{3,2,1,0:T(8,128)(2,1)S(1)}, bf16[2,4,128,256]{3,2,1,0:T(8,128)(2,1)}, u32[]{:S(2)}) copy-start(bf16[2,4,128,256]{3,2,1,0:T(8,128)(2,1)} %copy-done.4) | copy-start | bytes 1572868
  38.6 1.3 %copy-start.7 = (bf16[9,256,256]{2,1,0:T(8,128)(2,1)S(1)}, bf16[9,256,256]{2,1,0:T(8,128)(2,1)}, u32[]{:S(2)}) copy-start(bf16[9,256,256]{2,1,0:T(8,128)(2,1)} %param.5) | copy-start | bytes 3538948
  42.2 1.0 %copy-start.15 = (f32[256,256,1,1]{0,1,3,2:T(8,128)S(1)}, f32[256,256,1,1]{0,1,3,2:T(8,128)}, u32[]{:S(2)}) copy-start(f32[256,256,1,1]{0,1,3,2:T(8,128)} %fusion.106) | copy-start | bytes 786436
  43.3 4.5 %copy-start.9 = (f32[1024,256]{1,0:T(8,128)S(1)}, f32[1024,256]{1,0:T(8,128)}, u32[]{:S(2)}) copy-start(f32[1024,256]{1,0:T(8,128)} %copy-done.8) | copy-start | bytes 3145732
  43.4 4.5 %copy-start.11 = (f32[1024,256]{1,0:T(8,128)S(1)}, f32[1024,256]{1,0:T(8,128)}, u32[]{:S(2)}) copy-start(f32[1024,256]{1,0:T(8,128)} %copy-done.10) | copy-start | bytes 3145732
  43.4 6.1 %collective-permute-start.6 = (bf16[12,8,16,256]{3,2,1,0:T(8,128)(2,1)S(1)}, bf16[12,8,16,256]{3,2,1,0:T(8,128)(2,1)S(1)}, u32[]{:S(2)}, u32[]{:S(2)}) collective-permute-start(bf16[12,8,16,256]{3,2,1,0:T(8,128)(2,1)S(1)} %fusion.23), channel_id=1, source_target_pairs={{0,1},{1,0},{2,3},{3,2},{4,5},{5,4},{6,7},{7,6},{8,9},{9,8},{10,11... | collective-permute-start | bytes 2359304 | tf_op jit(solution)/shard_map/ppermute | solution.py:53
  49.8 11.5 %collective-permute-start.7 = (bf16[12,8,16,128]{3,2,1,0:T(8,128)(2,1)S(1)}, bf16[12,8,16,128]{3,2,1,0:T(8,128)(2,1)S(1)}, u32[]{:S(2)}, u32[]{:S(2)}) collective-permute-start(bf16[12,8,16,128]{3,2,1,0:T(8,128)(2,1)S(1)} %select_convert_fusion), channel_id=1, source_target_pairs={{0,16},{16,0},{1,17},{17,1},{2,18},{18,2},{3,19},{19,3},{4,20},{20... | collective-permute-start | bytes 1179656 | tf_op jit(solution)/shard_map/ppermute | solution.py:53
  61.5 6.5 %collective-permute-start.8 = (bf16[12,4,16,128]{3,2,1,0:T(8,128)(2,1)S(1)}, bf16[12,4,16,128]{3,2,1,0:T(8,128)(2,1)S(1)}, u32[]{:S(2)}, u32[]{:S(2)}) collective-permute-start(bf16[12,4,16,128]{3,2,1,0:T(8,128)(2,1)S(1)} %fusion.35), channel_id=1, source_target_pairs={{0,2},{1,3},{2,0},{3,1},{4,6},{5,7},{6,4},{7,5},{8,10},{9,11},{10,... | collective-permute-start | bytes 589832 | tf_op jit(solution)/shard_map/ppermute | solution.py:53
  64.4 6.0 %copy-start.13 = (bf16[3,256,256]{2,1,0:T(8,128)(2,1)S(1)}, bf16[3,256,256]{2,1,0:T(8,128)(2,1)}, u32[]{:S(2)}) copy-start(bf16[3,256,256]{2,1,0:T(8,128)(2,1)} %param.6) | copy-start | bytes 1179652
  64.4 12.0 %copy-start.14 = (f32[1024,256]{1,0:T(8,128)S(1)}, f32[1024,256]{1,0:T(8,128)}, u32[]{:S(2)}) copy-start(f32[1024,256]{1,0:T(8,128)} %fusion.34) | copy-start | bytes 3145732
  68.2 4.8 %collective-permute-start.9 = (bf16[12,2,16,128]{3,2,1,0:T(8,128)(2,1)S(1)}, bf16[12,2,16,128]{3,2,1,0:T(8,128)(2,1)S(1)}, u32[]{:S(2)}, u32[]{:S(2)}) collective-permute-start(bf16[12,2,16,128]{3,2,1,0:T(8,128)(2,1)S(1)} %fusion.91), channel_id=1, source_target_pairs={{0,4},{1,5},{2,6},{3,7},{4,0},{5,1},{6,2},{7,3},{8,12},{9,13},{10,... | collective-permute-start | bytes 294920 | tf_op jit(solution)/shard_map/ppermute | solution.py:53
  73.0 5.5 %collective-permute-start.10 = (bf16[12,1,16,128]{3,2,1,0:T(8,128)(2,1)S(1)}, bf16[12,1,16,128]{3,2,1,0:T(8,128)(2,1)S(1)}, u32[]{:S(2)}, u32[]{:S(2)}) collective-permute-start(bf16[12,1,16,128]{3,2,1,0:T(8,128)(2,1)S(1)} %dynamic-slice_convert_fusion.2), channel_id=1, source_target_pairs={{0,8},{1,9},{2,10},{3,11},{4,12},{5,13},{6,14},{7,15},{8,0},{9,1},... | collective-permute-start | bytes 147464 | tf_op jit(solution)/shard_map/ppermute | solution.py:53

commit v2 on v1

--- a/solution.py
+++ b/solution.py
@@ -1,6 +1,10 @@
+import functools
+
 import jax
 import jax.numpy as jnp
 from jax import lax
+from jax.experimental import pallas as pl
+from jax.experimental.pallas import tpu as pltpu
 from jax.sharding import PartitionSpec as P
 
 
@@ -48,44 +52,145 @@
     return back_sum.reshape(grad_ext[0:count].shape).astype(jnp.bfloat16)
 
 
-def exchange(keep, send, axis, step):
-    count = lax.axis_size(axis)
-    got = lax.ppermute(send.astype(jnp.bfloat16), axis, [(i, i ^ step) for i in range(count)])
-    return keep + got.astype(jnp.float32)
-
-
-def halve_chunks(sums, axis, step):
-    taps, chunks, rows, width = sums.shape
-    pairs = sums.reshape(taps, chunks // 2, 2, rows, width)
-    mine = lax.rem(lax.axis_index(axis) // step, 2)
-    keep = lax.dynamic_index_in_dim(pairs, mine, 2, keepdims=False)
-    send = lax.dynamic_index_in_dim(pairs, 1 - mine, 2, keepdims=False)
-    return exchange(keep, send, axis, step)
-
-
-def halve_width(sums, axis, step):
-    half = sums.shape[3] // 2
-    mine = lax.rem(lax.axis_index(axis) // step, 2)
-    low, high = sums[..., :half], sums[..., half:]
-    keep = jnp.where(mine == 0, low, high)
-    send = jnp.where(mine == 0, high, low)
-    return exchange(keep, send, axis, step)
+MESH = pl.DeviceIdType.MESH
+
+
+def bit_orders(bands, groups):
+    frame_bits = [("tm", 1 << i, 1 << i) for i in range(groups.bit_length() - 1)]
+    row_bits = [("space", 1 << i, groups << i) for i in range(bands.bit_length() - 1)]
+    first, second, rest = row_bits[:1], row_bits[1:2], row_bits[2:]
+    return [
+        first + frame_bits + second + rest,
+        first + second + rest + frame_bits,
+        first + rest + frame_bits + second,
+    ]
+
+
+def side(bit):
+    axis, step, _ = bit
+    return lax.rem(lax.axis_index(axis) // step, 2)
+
+
+def partner(bit):
+    axis, step, _ = bit
+    at = {"tm": lax.axis_index("tm"), "space": lax.axis_index("space")}
+    at[axis] = at[axis] + step - 2 * step * side(bit)
+    return (at["tm"], at["space"])
+
+
+def each(count, step):
+    if count <= 16:
+        for e in range(count):
+            step(e)
+    else:
+        lax.fori_loop(0, count, lambda e, carry: (step(e), carry)[1], 0)
+
+
+def spread(e, free):
+    if isinstance(e, int):
+        return sum(((e >> i) % 2) * bit[2] for i, bit in enumerate(free))
+    total = 0
+    for i, bit in enumerate(free):
+        total = total + lax.rem(e // (1 << i), 2) * bit[2]
+    return total
+
+
+def scatter_kernel(orders, sums_ref, out_ref, total, sent, landed, send_sems, recv_sems):
+    parts = len(orders)
+    rows = sums_ref.shape[1] // parts
+    stages = len(orders[0])
+    barrier = pltpu.get_barrier_semaphore()
+    for bit in orders[0]:
+        pl.semaphore_signal(barrier, inc=1, device_id=partner(bit), device_id_type=MESH)
+    pl.semaphore_wait(barrier, stages)
+
+    def span(part):
+        return pl.ds(part * rows, rows)
+
+    def start_of(stage):
+        return sum(1 << (stages - 1 - s) for s in range(stage))
+
+    def fixed(part, stage):
+        return sum(side(bit) * bit[2] for bit in orders[part][:stage])
+
+    def send(part, stage):
+        bit, free = orders[part][stage], orders[part][stage + 1 :]
+        count, start = 1 << len(free), start_of(stage)
+        base = fixed(part, stage) + (1 - side(bit)) * bit[2]
+        source = sums_ref if stage == 0 else total
+
+        def pack(e):
+            block = source[base + spread(e, free), span(part), :]
+            sent[part, start + e] = block.astype(jnp.bfloat16)
+
+        each(count, pack)
+        copy = pltpu.make_async_remote_copy(
+            src_ref=sent.at[part, pl.ds(start, count)],
+            dst_ref=landed.at[part, pl.ds(start, count)],
+            send_sem=send_sems.at[part, stage],
+            recv_sem=recv_sems.at[part, stage],
+            device_id=partner(bit),
+            device_id_type=MESH,
+        )
+        copy.start()
+        return copy
+
+    def add(part, stage):
+        free = orders[part][stage + 1 :]
+        count, start = 1 << len(free), start_of(stage)
+        base = fixed(part, stage + 1)
+        source = sums_ref if stage == 0 else total
+
+        def step(e):
+            at = base + spread(e, free)
+            got = landed[part, start + e].astype(jnp.float32)
+            total[at, span(part), :] = source[at, span(part), :] + got
+
+        each(count, step)
+
+    copies = [send(part, 0) for part in range(parts)]
+    for stage in range(stages):
+        for part in range(parts):
+            copies[part].wait_recv()
+            add(part, stage)
+            copies[part].wait_send()
+            if stage + 1 < stages:
+                copies[part] = send(part, stage + 1)
+            else:
+                out_ref[span(part), :] = total[fixed(part, stages), span(part), :]
 
 
 def scatter_sums(sums):
     bands, groups = lax.axis_size("space"), lax.axis_size("tm")
     taps, rows, width = sums.shape
-    sums = sums.reshape(taps, bands, rows // bands, width)
-    sums = halve_chunks(sums, "space", 1)
-    step = groups // 2
-    while step >= 1:
-        sums = halve_width(sums, "tm", step)
-        step //= 2
-    step = 2
-    while step < bands:
-        sums = halve_chunks(sums, "space", step)
-        step *= 2
-    return jnp.transpose(sums[:, 0], (0, 2, 1))
+    depth, lanes = rows // bands, width // groups
+    size = taps * depth * lanes
+    blocks = sums.reshape(taps, bands, depth, groups, lanes).transpose(1, 3, 0, 2, 4)
+    blocks = blocks.reshape(bands * groups, size // 128, 128)
+    lines = -(-size // 128 // 16) * 16
+    blocks = jnp.pad(blocks, ((0, 0), (0, lines - size // 128), (0, 0)))
+    orders = bit_orders(bands, groups)
+    if lines % 48:
+        orders = orders[:1]
+    parts, stages, devices = len(orders), len(orders[0]), bands * groups
+    owned = pl.pallas_call(
+        functools.partial(scatter_kernel, orders),
+        out_shape=jax.ShapeDtypeStruct((lines, 128), jnp.float32),
+        in_specs=[pl.BlockSpec(memory_space=pltpu.VMEM)],
+        out_specs=pl.BlockSpec(memory_space=pltpu.VMEM),
+        scratch_shapes=[
+            pltpu.VMEM((devices, lines, 128), jnp.float32),
+            pltpu.VMEM((parts, devices, lines // parts, 128), jnp.bfloat16),
+            pltpu.VMEM((parts, devices, lines // parts, 128), jnp.bfloat16),
+            pltpu.SemaphoreType.DMA((parts, stages)),
+            pltpu.SemaphoreType.DMA((parts, stages)),
+        ],
+        compiler_params=pltpu.CompilerParams(
+            collective_id=0, has_side_effects=True, vmem_limit_bytes=24 * 1024 * 1024
+        ),
+    )(blocks)
+    owned = owned[: size // 128].reshape(taps, depth, lanes)
+    return jnp.transpose(owned, (0, 2, 1))
 
 
 def body(frames_in, w_space, w_time, grad_out):

time: 80.3 us -> 144 us (1.79)
  local copies, waits for them, and re-layouts: 8.61 us -> 64.7 us
  Pallas kernels: 0 us -> 24.9 us
  waiting for transfers between devices: 23.6 us -> 0.02 us
  matrix products: 18.4 us -> 30.4 us
  starting transfers between devices: 24.2 us -> 16.5 us
  other arithmetic: 3.67 us -> 5.28 us
    pallas_call x0 -> x1, Pallas kernels: none -> 24.9 us  [scatter_sums(): pl.pallas_call(functools.partial(scatter_kernel, orders), out_shape=jax.S...]
    ppermute x5 -> x0, waiting for transfers between devices: 18.4 us -> none  [exchange(): lax.ppermute(send.astype(jnp.bfloat16), axis, [(i, i ^ step) for i in ran...]
    slice x1 -> x9, local copies, waits for them, and re-layouts: 0.42 us -> 18.1 us  [body(): grad_ext_rows[:, 2 - i:2 - i + height, 2 - j:2 - j + width]]
    dot_general x1 -> x10, local copies, waits for them, and re-layouts: 1 us -> 17.1 us  [body(): lax.dot_general(flat_pre, source, (((0,), (0,)), ((), ())), preferred_ele...]
    unnamed x34 -> x91, local copies, waits for them, and re-layouts: 3.49 us -> 16.6 us
    ppermute x5 -> x0, starting transfers between devices: 11.5 us -> none  [exchange(): lax.ppermute(send.astype(jnp.bfloat16), axis, [(i, i ^ step) for i in ran...]
    dot_general x9, matrix products: 5.14 us -> 9.42 us  [body(): lax.dot_general(flat_pre, source, (((0,), (0,)), ((), ())), preferred_ele...]
    ppermute x1, waiting for transfers between devices: 3.95 us -> 0.01 us  [body(): grad_next = lax.ppermute(grad_out[:2], 'tm', [(t, s) for s, t in onward])]
  transfers between devices with their start and end apart: 11 -> 6, of which waited for: 7 -> 0; matrix products, arithmetic and copies ran while one was open for 27% -> 54% of each run, Pallas kernels for 0% -> 0%
where the time goes in v2:
time: 144 us; the launch traced here: 143 us
  local copies, waits for them, and re-layouts  64.7 us (45%)
  matrix products  30.4 us (21%)
  Pallas kernels  24.9 us (17%)
  starting transfers between devices  16.5 us (11%)
  other arithmetic  5.28 us (4%)
    pallas_call x1, Pallas kernels, scatter_sums(): pl.pallas_call(functools.partial(scatter_kernel, orders), out_shape=jax.S...  24.9 us
    slice x9, local copies, waits for them, and re-layouts, body(): grad_ext_rows[:, 2 - i:2 - i + height, 2 - j:2 - j + width]  18.1 us
    dot_general x10, local copies, waits for them, and re-layouts, body(): lax.dot_general(flat_pre, source, (((0,), (0,)), ((), ())), preferred_ele...  17.1 us
    unnamed x91, local copies, waits for them, and re-layouts  16.6 us
    dot_general x9, matrix products, body(): lax.dot_general(flat_pre, source, (((0,), (0,)), ((), ())), preferred_ele...  9.42 us
    dot_general x9, matrix products, body(): lax.dot_general(window, w_space[3 * i + j], (((1,), (1,)), ((), ())), pre...  7.22 us
    ppermute x2, starting transfers between devices, extended_2(): lax.ppermute(lax.slice_in_dim(block, block.shape[dim] - width, None, axis...  7.07 us
    ppermute x1, starting transfers between devices, body(): past = lax.ppermute(hidden[count - 2:], 'tm', onward)  5.4 us
  transfers between devices with their start and end apart: 6, of which 0 were waited for; matrix products, arithmetic and copies ran while one was open for 54% of the time, Pallas kernels for 0%

profile of v2, /device:TPU:0, one launch (start us, length us, event | category | flops | bytes accessed | tf_op | source)
XLA Modules:
  0.0 143.0 jit_solution(13870476694373966718)
XLA Ops:
  1.7 2.4 %collective-permute-start = (bf16[2,1,128,256]{3,2,1,0:T(8,128)(2,1)S(1)}, bf16[2,1,128,256]{3,2,1,0:T(8,128)(2,1)S(1)}, u32[]{:S(2)}, u32[]{:S(2)}) collective-permute-start(bf16[2,1,128,256]{3,2,1,0:T(8,128)(2,1)S(1)} %get-tuple-element.30), channel_id=1, source_target_pairs={{0,1},{1,2},{2,3},{3,4},{4,5},{5,6},{6,7},{7,8},{8,9},{9,10},{10,1... | collective-permute-start | bytes 393224 | tf_op jit(solution)/shard_map/ppermute | solution.py:16
  6.7 2.4 %fusion.42 = f32[1024,256]{1,0:T(8,128)} fusion(bf16[1024,256]{1,0:T(8,128)(2,1)} %bitcast.232, bf16[3,256,256]{2,1,0:T(8,128)(2,1)} %param.6), kind=kOutput, calls=%fused_computation.89 | convolution fusion | flops 134217728 | bytes 1703936 | tf_op jit(solution)/shard_map/dot_general | solution.py:49
  12.3 2.6 %slice_bitcast_fusion = (bf16[256,2,4,128]{0,3,2,1:T(8,128)(2,1)}, bf16[256,2,4,128]{0,3,2,1:T(8,128)(2,1)}, bf16[256,2,4,128]{0,3,2,1:T(8,128)(2,1)}, bf16[256,...) fusion(bf16[2,6,130,256]{3,2,1,0:T(8,128)(2,1)S(1)} %fusion.21), kind=kLoop, calls=%fused_computation.156 | loop fusion | bytes 9437184 | tf_op jit(solution)/shard_map/dot_general | solution.py:224
  14.9 2.1 %copy.104 = bf16[256,2,4,128]{3,0,2,1:T(8,128)(2,1)} copy(bf16[256,2,4,128]{0,3,2,1:T(8,128)(2,1)} %get-tuple-element.12) | data formatting | bytes 1048576 | tf_op jit(solution)/shard_map/dot_general | solution.py:224
  17.0 2.0 %copy.81 = bf16[256,2,4,128]{3,0,2,1:T(8,128)(2,1)} copy(bf16[256,2,4,128]{0,3,2,1:T(8,128)(2,1)} %get-tuple-element.13) | data formatting | bytes 1048576 | tf_op jit(solution)/shard_map/dot_general | solution.py:224
  20.1 2.2 %copy.90 = bf16[256,2,4,128]{3,0,2,1:T(8,128)(2,1)} copy(bf16[256,2,4,128]{0,3,2,1:T(8,128)(2,1)} %get-tuple-element.15) | data formatting | bytes 1048576 | tf_op jit(solution)/shard_map/dot_general | solution.py:224
  22.3 2.1 %copy.95 = bf16[256,2,4,128]{3,0,2,1:T(8,128)(2,1)} copy(bf16[256,2,4,128]{0,3,2,1:T(8,128)(2,1)} %get-tuple-element.16) | data formatting | bytes 1048576 | tf_op jit(solution)/shard_map/dot_general | solution.py:224
  24.3 2.1 %copy.98 = bf16[256,2,4,128]{3,0,2,1:T(8,128)(2,1)} copy(bf16[256,2,4,128]{0,3,2,1:T(8,128)(2,1)} %get-tuple-element.17) | data formatting | bytes 1048576 | tf_op jit(solution)/shard_map/dot_general | solution.py:224
  31.5 1.4 fusion.9
  32.8 2.7 %copy.68 = f32[2,4,128,256]{2,3,1,0:T(8,128)} copy(f32[2,4,128,256]{3,2,1,0:T(8,128)} %bitcast.248) | data formatting | bytes 2097152 | tf_op jit(solution)/shard_map/reshape | solution.py:207
  35.5 1.4 fusion.41
  38.3 1.4 fusion.12
  42.0 2.0 %multiply_convert_fusion.1 = (bf16[2,4,128,256]{2,3,1,0:T(8,128)(2,1)S(1)}, bf16[2,4,128,256]{2,3,1,0:T(8,128)(2,1)S(1)}) fusion(f32[2,4,128,256]{2,3,1,0:T(8,128)} %copy.68, f32[2,4,128,256]{2,3,1,0:T(8,128)} %copy.71), kind=kLoop, calls=%fused_computation.41 | loop fusion | flops 2883584 | bytes 3145728 | tf_op jit(solution)/shard_map/convert_element_type | solution.py:214
  44.4 5.4 %collective-permute-start.2 = (bf16[2,4,128,256]{2,3,1,0:T(8,128)(2,1)S(1)}, bf16[2,4,128,256]{2,3,1,0:T(8,128)(2,1)S(1)}, u32[]{:S(2)}, u32[]{:S(2)}) collective-permute-start(bf16[2,4,128,256]{2,3,1,0:T(8,128)(2,1)S(1)} %get-tuple-element.11), channel_id=1, source_target_pairs={{0,16},{1,17},{2,18},{3,19},{4,20},{5,21},{6,22},{7,23},{8,24},{9,... | collective-permute-start | bytes 1572872 | tf_op jit(solution)/shard_map/ppermute | solution.py:209
  62.0 4.7 %collective-permute-start.4 = (bf16[2,1,128,256]{2,3,1,0:T(8,128)(2,1)}, bf16[2,1,128,256]{2,3,1,0:T(8,128)(2,1)S(1)}, u32[]{:S(2)}, u32[]{:S(2)}) collective-permute-start(bf16[2,1,128,256]{2,3,1,0:T(8,128)(2,1)} %get-tuple-element.26), channel_id=1, source_target_pairs={{0,1},{1,2},{2,3},{3,4},{4,5},{5,6},{6,7},{7,8},{8,9},{9,10},{10,1... | collective-permute-start | bytes 393224 | tf_op jit(solution)/shard_map/ppermute | solution.py:16
  66.7 1.5 %collective-permute-start.5 = (bf16[2,1,128,256]{2,3,1,0:T(8,128)(2,1)}, bf16[2,1,128,256]{2,3,1,0:T(8,128)(2,1)S(1)}, u32[]{:S(2)}, u32[]{:S(2)}) collective-permute-start(bf16[2,1,128,256]{2,3,1,0:T(8,128)(2,1)} %get-tuple-element.27), channel_id=1, source_target_pairs={{1,0},{2,1},{3,2},{4,3},{5,4},{6,5},{7,6},{8,7},{9,8},{10,9},{11,1... | collective-permute-start | bytes 393224 | tf_op jit(solution)/shard_map/ppermute | solution.py:19
  68.2 1.7 %bitcast_dynamic-update-slice_fusion.8 = f32[12,16,16,2,128]{4,2,1,3,0:T(8,128)} fusion(f32[16,16,2,128,1,1]{3,1,5,2,0,4:T(8,128)} %fusion.38), kind=kLoop, calls=%fused_computation.85 | loop fusion | bytes 524288
  69.8 1.7 %bitcast_dynamic-update-slice_fusion.7 = f32[12,16,16,2,128]{4,2,1,3,0:T(8,128)} fusion(f32[12,16,16,2,128]{4,2,1,3,0:T(8,128)} %bitcast_dynamic-update-slice_fusion.8, f32[16,16,2,128,1,1]{3,1,5,2,0,4:T(8,128)} %fusion.36), kind=kLoop, calls=%fused_computation.84 | loop fusion | bytes 524288
  71.6 1.7 %bitcast_dynamic-update-slice_fusion.6 = f32[12,16,16,2,128]{4,2,1,3,0:T(8,128)} fusion(f32[12,16,16,2,128]{4,2,1,3,0:T(8,128)} %bitcast_dynamic-update-slice_fusion.7, f32[16,16,2,128,1,1]{3,1,5,2,0,4:T(8,128)} %fusion.34), kind=kLoop, calls=%fused_computation.83 | loop fusion | bytes 524288
  79.3 2.1 %copy.79 = bf16[2,4,128,256]{3,2,1,0:T(8,128)(2,1)} copy(bf16[2,4,128,256]{2,3,1,0:T(8,128)(2,1)} %get-tuple-element.24) | data formatting | bytes 1048576 | tf_op jit(solution)/shard_map/slice | solution.py:235
  81.4 2.0 %copy.74 = bf16[2,4,128,256]{3,2,1,0:T(8,128)(2,1)} copy(bf16[2,4,128,256]{2,3,1,0:T(8,128)(2,1)} %get-tuple-element.25) | data formatting | bytes 1048576 | tf_op jit(solution)/shard_map/slice | solution.py:235
  83.5 2.4 %fusion.66 = f32[1024,256]{1,0:T(8,128)} fusion(bf16[1024,256]{1,0:T(8,128)(2,1)} %bitcast.259, bf16[9,256,256]{2,1,0:T(8,128)(2,1)S(1)} %copy-done.2), kind=kOutput, calls=%fused_computation.113 | convolution fusion | flops 134217728 | bytes 1703936 | tf_op jit(solution)/shard_map/dot_general | solution.py:238
  86.6 2.5 %fusion.109 = (bf16[2,4,128,256]{2,3,1,0:T(8,128)(2,1)}, bf16[2,4,128,256]{2,3,1,0:T(8,128)(2,1)}, bf16[2,4,128,256]{2,3,1,0:T(8,128)(2,1)}, bf16[2,4,128,256]{2...) fusion(bf16[2,6,130,256]{2,3,1,0:T(8,128)(2,1)S(1)} %fusion.6), kind=kLoop, calls=%fused_computation.162 | loop fusion | bytes 6291456 | tf_op jit(solution)/shard_map/slice | solution.py:235
  90.4 2.1 %copy.78 = bf16[2,4,128,256]{3,2,1,0:T(8,128)(2,1)} copy(bf16[2,4,128,256]{2,3,1,0:T(8,128)(2,1)} %get-tuple-element.5) | data formatting | bytes 1048576 | tf_op jit(solution)/shard_map/slice | solution.py:235
  92.5 2.1 %copy.77 = bf16[2,4,128,256]{3,2,1,0:T(8,128)(2,1)} copy(bf16[2,4,128,256]{2,3,1,0:T(8,128)(2,1)} %get-tuple-element.6) | data formatting | bytes 1048576 | tf_op jit(solution)/shard_map/slice | solution.py:235
  94.6 2.0 %copy.76 = bf16[2,4,128,256]{3,2,1,0:T(8,128)(2,1)} copy(bf16[2,4,128,256]{2,3,1,0:T(8,128)(2,1)} %get-tuple-element.7) | data formatting | bytes 1048576 | tf_op jit(solution)/shard_map/slice | solution.py:235
  96.6 2.0 %copy.75 = bf16[2,4,128,256]{3,2,1,0:T(8,128)(2,1)} copy(bf16[2,4,128,256]{2,3,1,0:T(8,128)(2,1)} %get-tuple-element.8) | data formatting | bytes 1048576 | tf_op jit(solution)/shard_map/slice | solution.py:235
  98.6 2.0 %copy.73 = bf16[2,4,128,256]{3,2,1,0:T(8,128)(2,1)} copy(bf16[2,4,128,256]{2,3,1,0:T(8,128)(2,1)} %get-tuple-element.9) | data formatting | bytes 1048576 | tf_op jit(solution)/shard_map/slice | solution.py:235
  100.7 1.5 %fusion.69 = f32[1024,256]{1,0:T(8,128)S(1)} fusion(bf16[1024,256]{1,0:T(8,128)(2,1)} %bitcast.260, bf16[9,256,256]{2,1,0:T(8,128)(2,1)S(1)} %copy-done.2), kind=kOutput, calls=%fused_computation.116 | convolution fusion | flops 134217728 | bytes 1703936 | tf_op jit(solution)/shard_map/dot_general | solution.py:238
  111.4 2.3 %copy.113 = f32[16,2,12,16,128]{4,3,2,1,0:T(8,128)S(1)} copy(f32[16,2,12,16,128]{4,3,0,1,2:T(8,128)} %bitcast.103) | data formatting | bytes 6291456 | tf_op jit(solution)/shard_map/transpose | solution.py:168
  113.7 24.9 %shard_map.75 = f32[192,128]{1,0:T(8,128)S(1)} custom-call(f32[32,192,128]{2,1,0:T(8,128)S(1)} %bitcast.229), custom_call_target="tpu_custom_call" | custom-call | tf_op jit(solution)/shard_map/pallas_call | solution.py:176
  140.7 2.3 %fusion.10 = bf16[1024,256]{1,0:T(8,128)(2,1)} fusion(f32[1024,256]{1,0:T(8,128)} %fusion.41, f32[1024,256]{1,0:T(8,128)S(1)} %fusion.47, bf16[1024,256]{1,0:T(8,128)(2,1)S(1)} %bitcast.253, bf16[3,256,256]{2,1,0:T(8,128)(2,1)S(1)} %copy-done.20), kind=kOutput, calls=%fused_computation.30 | convolution fusion | flops 135004160 | bytes 3276800 | tf_op jit(solution)/shard_map/dot_general | solution.py:35
  (150 shorter events, 48.1 us)
Async XLA Ops:
  0.6 8.4 %copy-start.1 = (bf16[2,4,128,256]{3,2,1,0:T(8,128)(2,1)S(1)}, bf16[2,4,128,256]{3,2,1,0:T(8,128)(2,1)}, u32[]{:S(2)}) copy-start(bf16[2,4,128,256]{3,2,1,0:T(8,128)(2,1)} %param.4) | copy-start | bytes 1572868
  1.7 8.3 %collective-permute-start = (bf16[2,1,128,256]{3,2,1,0:T(8,128)(2,1)S(1)}, bf16[2,1,128,256]{3,2,1,0:T(8,128)(2,1)S(1)}, u32[]{:S(2)}, u32[]{:S(2)}) collective-permute-start(bf16[2,1,128,256]{3,2,1,0:T(8,128)(2,1)S(1)} %get-tuple-element.30), channel_id=1, source_target_pairs={{0,1},{1,2},{2,3},{3,4},{4,5},{5,6},{6,7},{7,8},{8,9},{9,10},{10,1... | collective-permute-start | bytes 393224 | tf_op jit(solution)/shard_map/ppermute | solution.py:16
  4.1 5.9 %collective-permute-start.1 = (bf16[2,1,128,256]{3,2,1,0:T(8,128)(2,1)S(1)}, bf16[2,1,128,256]{3,2,1,0:T(8,128)(2,1)S(1)}, u32[]{:S(2)}, u32[]{:S(2)}) collective-permute-start(bf16[2,1,128,256]{3,2,1,0:T(8,128)(2,1)S(1)} %get-tuple-element.31), channel_id=1, source_target_pairs={{1,0},{2,1},{3,2},{4,3},{5,4},{6,5},{7,6},{8,7},{9,8},{10,9},{11,1... | collective-permute-start | bytes 393224 | tf_op jit(solution)/shard_map/ppermute | solution.py:19
  5.4 31.5 %collective-permute-start.3 = (bf16[2,4,128,256]{3,2,1,0:T(8,128)(2,1)}, bf16[2,4,128,256]{3,2,1,0:T(8,128)(2,1)}, u32[]{:S(2)}, u32[]{:S(2)}) collective-permute-start(bf16[2,4,128,256]{3,2,1,0:T(8,128)(2,1)} %param.7), channel_id=1, source_target_pairs={{16,0},{17,1},{18,2},{19,3},{20,4},{21,5},{22,6},{23,7},{24,8},{25... | collective-permute-start | bytes 1572872 | tf_op jit(solution)/shard_map/ppermute | solution.py:200
  14.9 4.2 %copy-start.9 = (bf16[256,2,4,128]{0,3,2,1:T(8,128)(2,1)S(1)}, bf16[256,2,4,128]{0,3,2,1:T(8,128)(2,1)}, u32[]{:S(2)}) copy-start(bf16[256,2,4,128]{0,3,2,1:T(8,128)(2,1)} %get-tuple-element.14) | copy-start | bytes 1572868
  20.1 6.3 %copy-start.2 = (bf16[9,256,256]{2,1,0:T(8,128)(2,1)S(1)}, bf16[9,256,256]{2,1,0:T(8,128)(2,1)}, u32[]{:S(2)}) copy-start(bf16[9,256,256]{2,1,0:T(8,128)(2,1)} %param.5) | copy-start | bytes 3538948
  32.8 2.7 %copy-start.3 = (f32[1024,256]{1,0:T(8,128)S(1)}, f32[1024,256]{1,0:T(8,128)}, u32[]{:S(2)}) copy-start(f32[1024,256]{1,0:T(8,128)} %fusion.9) | copy-start | bytes 3145732
  32.8 2.7 %copy-start.19 = (bf16[3,256,256]{2,1,0:T(8,128)(2,1)S(1)}, bf16[3,256,256]{2,1,0:T(8,128)(2,1)}, u32[]{:S(2)}) copy-start(bf16[3,256,256]{2,1,0:T(8,128)(2,1)} %param.6) | copy-start | bytes 1179652
  44.1 6.5 %copy-start.27 = (bf16[256,2,4,128]{3,0,2,1:T(8,128)(2,1)S(1)}, bf16[256,2,4,128]{3,0,2,1:T(8,128)(2,1)}, u32[]{:S(2)}) copy-start(bf16[256,2,4,128]{3,0,2,1:T(8,128)(2,1)} %copy.84) | copy-start | bytes 1572868
  44.1 7.5 %copy-start.32 = (bf16[256,2,4,128]{3,0,2,1:T(8,128)(2,1)S(1)}, bf16[256,2,4,128]{3,0,2,1:T(8,128)(2,1)}, u32[]{:S(2)}) copy-start(bf16[256,2,4,128]{3,0,2,1:T(8,128)(2,1)} %copy.87) | copy-start | bytes 1572868
  44.4 63.6 %collective-permute-start.2 = (bf16[2,4,128,256]{2,3,1,0:T(8,128)(2,1)S(1)}, bf16[2,4,128,256]{2,3,1,0:T(8,128)(2,1)S(1)}, u32[]{:S(2)}, u32[]{:S(2)}) collective-permute-start(bf16[2,4,128,256]{2,3,1,0:T(8,128)(2,1)S(1)} %get-tuple-element.11), channel_id=1, source_target_pairs={{0,16},{1,17},{2,18},{3,19},{4,20},{5,21},{6,22},{7,23},{8,24},{9,... | collective-permute-start | bytes 1572872 | tf_op jit(solution)/shard_map/ppermute | solution.py:209
  50.6 2.1 %copy-start.33 = (bf16[256,2,4,128]{3,0,2,1:T(8,128)(2,1)S(1)}, bf16[256,2,4,128]{3,0,2,1:T(8,128)(2,1)}, u32[]{:S(2)}) copy-start(bf16[256,2,4,128]{3,0,2,1:T(8,128)(2,1)} %copy.90) | copy-start | bytes 1572868
  51.6 2.1 %copy-start.25 = (bf16[2,128,2,4,128]{1,0,4,3,2:T(2,128)(2,1)S(1)}, bf16[2,128,2,4,128]{1,0,4,3,2:T(2,128)(2,1)}, u32[]{:S(2)}) copy-start(bf16[2,128,2,4,128]{1,0,4,3,2:T(2,128)(2,1)} %dot_general.212) | copy-start | bytes 1572868
  52.6 2.1 %copy-start.30 = (bf16[256,2,4,128]{3,0,2,1:T(8,128)(2,1)S(1)}, bf16[256,2,4,128]{3,0,2,1:T(8,128)(2,1)}, u32[]{:S(2)}) copy-start(bf16[256,2,4,128]{3,0,2,1:T(8,128)(2,1)} %copy.95) | copy-start | bytes 1572868
  53.7 2.1 %copy-start.31 = (bf16[256,2,4,128]{3,0,2,1:T(8,128)(2,1)S(1)}, bf16[256,2,4,128]{3,0,2,1:T(8,128)(2,1)}, u32[]{:S(2)}) copy-start(bf16[256,2,4,128]{3,0,2,1:T(8,128)(2,1)} %copy.98) | copy-start | bytes 1572868
  54.7 2.1 %copy-start.26 = (bf16[256,2,4,128]{3,0,2,1:T(8,128)(2,1)S(1)}, bf16[256,2,4,128]{3,0,2,1:T(8,128)(2,1)}, u32[]{:S(2)}) copy-start(bf16[256,2,4,128]{3,0,2,1:T(8,128)(2,1)} %copy.101) | copy-start | bytes 1572868
  55.8 2.1 %copy-start.28 = (bf16[256,2,4,128]{3,0,2,1:T(8,128)(2,1)S(1)}, bf16[256,2,4,128]{3,0,2,1:T(8,128)(2,1)}, u32[]{:S(2)}) copy-start(bf16[256,2,4,128]{3,0,2,1:T(8,128)(2,1)} %copy.104) | copy-start | bytes 1572868
  56.9 2.1 %copy-start.29 = (bf16[256,2,4,128]{3,0,2,1:T(8,128)(2,1)S(1)}, bf16[256,2,4,128]{3,0,2,1:T(8,128)(2,1)}, u32[]{:S(2)}) copy-start(bf16[256,2,4,128]{3,0,2,1:T(8,128)(2,1)} %copy.81) | copy-start | bytes 1572868
  61.9 11.4 %copy-start.39 = (f32[16,16,2,128,1,1]{3,1,5,2,0,4:T(8,128)S(1)}, f32[16,16,2,128,1,1]{3,1,5,2,0,4:T(8,128)}, u32[]{:S(2)}) copy-start(f32[16,16,2,128,1,1]{3,1,5,2,0,4:T(8,128)} %fusion.32) | copy-start | bytes 786436
  61.9 12.1 %copy-start.38 = (f32[16,16,2,128,1,1]{3,1,5,2,0,4:T(8,128)S(1)}, f32[16,16,2,128,1,1]{3,1,5,2,0,4:T(8,128)}, u32[]{:S(2)}) copy-start(f32[16,16,2,128,1,1]{3,1,5,2,0,4:T(8,128)} %fusion.30) | copy-start | bytes 786436
  62.0 12.8 %copy-start.37 = (f32[16,16,2,128,1,1]{3,1,5,2,0,4:T(8,128)S(1)}, f32[16,16,2,128,1,1]{3,1,5,2,0,4:T(8,128)}, u32[]{:S(2)}) copy-start(f32[16,16,2,128,1,1]{3,1,5,2,0,4:T(8,128)} %fusion.28) | copy-start | bytes 786436
  62.0 13.5 %copy-start.36 = (f32[16,16,2,128,1,1]{3,1,5,2,0,4:T(8,128)S(1)}, f32[16,16,2,128,1,1]{3,1,5,2,0,4:T(8,128)}, u32[]{:S(2)}) copy-start(f32[16,16,2,128,1,1]{3,1,5,2,0,4:T(8,128)} %fusion.26) | copy-start | bytes 786436
  62.0 15.7 %collective-permute-start.4 = (bf16[2,1,128,256]{2,3,1,0:T(8,128)(2,1)}, bf16[2,1,128,256]{2,3,1,0:T(8,128)(2,1)S(1)}, u32[]{:S(2)}, u32[]{:S(2)}) collective-permute-start(bf16[2,1,128,256]{2,3,1,0:T(8,128)(2,1)} %get-tuple-element.26), channel_id=1, source_target_pairs={{0,1},{1,2},{2,3},{3,4},{4,5},{5,6},{6,7},{7,8},{8,9},{9,10},{10,1... | collective-permute-start | bytes 393224 | tf_op jit(solution)/shard_map/ppermute | solution.py:16
  66.7 10.9 %collective-permute-start.5 = (bf16[2,1,128,256]{2,3,1,0:T(8,128)(2,1)}, bf16[2,1,128,256]{2,3,1,0:T(8,128)(2,1)S(1)}, u32[]{:S(2)}, u32[]{:S(2)}) collective-permute-start(bf16[2,1,128,256]{2,3,1,0:T(8,128)(2,1)} %get-tuple-element.27), channel_id=1, source_target_pairs={{1,0},{2,1},{3,2},{4,3},{5,4},{6,5},{7,6},{8,7},{9,8},{10,9},{11,1... | collective-permute-start | bytes 393224 | tf_op jit(solution)/shard_map/ppermute | solution.py:19
  69.8 6.3 %copy-start.35 = (f32[16,16,2,128,1,1]{3,1,5,2,0,4:T(8,128)S(1)}, f32[16,16,2,128,1,1]{3,1,5,2,0,4:T(8,128)}, u32[]{:S(2)}) copy-start(f32[16,16,2,128,1,1]{3,1,5,2,0,4:T(8,128)} %fusion.24) | copy-start | bytes 786436
  71.6 5.3 %copy-start.34 = (f32[16,16,2,128,1,1]{3,1,5,2,0,4:T(8,128)S(1)}, f32[16,16,2,128,1,1]{3,1,5,2,0,4:T(8,128)}, u32[]{:S(2)}) copy-start(f32[16,16,2,128,1,1]{3,1,5,2,0,4:T(8,128)} %fusion.22) | copy-start | bytes 786436
  83.5 2.4 %copy-start.22 = (bf16[2,1,128,256]{2,3,1,0:T(8,128)(2,1)S(1)}, bf16[2,1,128,256]{2,3,1,0:T(8,128)(2,1)}, u32[]{:S(2)}) copy-start(bf16[2,1,128,256]{2,3,1,0:T(8,128)(2,1)} %copy-done.21) | copy-start | bytes 393220
  83.5 2.4 %copy-start.24 = (bf16[2,1,128,256]{2,3,1,0:T(8,128)(2,1)S(1)}, bf16[2,1,128,256]{2,3,1,0:T(8,128)(2,1)}, u32[]{:S(2)}) copy-start(bf16[2,1,128,256]{2,3,1,0:T(8,128)(2,1)} %copy-done.23) | copy-start | bytes 393220
  100.7 1.5 %copy-start.8 = (f32[1024,256]{1,0:T(8,128)S(1)}, f32[1024,256]{1,0:T(8,128)}, u32[]{:S(2)}) copy-start(f32[1024,256]{1,0:T(8,128)} %fusion.66) | copy-start | bytes 3145732
  100.7 1.5 %copy-start.18 = (bf16[2,4,128,256]{3,2,1,0:T(8,128)(2,1)S(1)}, bf16[2,4,128,256]{3,2,1,0:T(8,128)(2,1)}, u32[]{:S(2)}) copy-start(bf16[2,4,128,256]{3,2,1,0:T(8,128)(2,1)} %copy.75) | copy-start | bytes 1572868
  102.5 1.6 %copy-start.6 = (f32[1024,256]{1,0:T(8,128)S(1)}, f32[1024,256]{1,0:T(8,128)}, u32[]{:S(2)}) copy-start(f32[1024,256]{1,0:T(8,128)} %copy-done.5) | copy-start | bytes 3145732
  138.6 1.5 %copy-start.20 = (bf16[3,256,256]{2,1,0:T(8,128)(2,1)S(1)}, bf16[3,256,256]{2,1,0:T(8,128)(2,1)}, u32[]{:S(2)}) copy-start(bf16[3,256,256]{2,1,0:T(8,128)(2,1)} %param.6) | copy-start | bytes 1179652
  (14 other events, 15.3 us)

commit v3 on v2

--- a/solution.py
+++ b/solution.py
@@ -95,9 +95,14 @@
     return total
 
 
-def scatter_kernel(orders, sums_ref, out_ref, total, sent, landed, send_sems, recv_sems):
+def scatter_kernel(orders, depth, lanes, *refs):
+    taps = len(refs) - 6
+    tap_refs = refs[:taps]
+    out_ref, total, sent, landed, send_sems, recv_sems = refs[taps:]
     parts = len(orders)
-    rows = sums_ref.shape[1] // parts
+    group = taps // parts
+    rows = group * depth
+    groups = lax.axis_size("tm")
     stages = len(orders[0])
     barrier = pltpu.get_barrier_semaphore()
     for bit in orders[0]:
@@ -107,6 +112,11 @@
     def span(part):
         return pl.ds(part * rows, rows)
 
+    def tap_block(part, k, at):
+        down = pl.multiple_of((at // groups) * depth, depth)
+        across = pl.multiple_of(lax.rem(at, groups) * lanes, lanes)
+        return tap_refs[part * group + k][pl.ds(down, depth), pl.ds(across, lanes)]
+
     def start_of(stage):
         return sum(1 << (stages - 1 - s) for s in range(stage))
 
@@ -117,11 +127,15 @@
         bit, free = orders[part][stage], orders[part][stage + 1 :]
         count, start = 1 << len(free), start_of(stage)
         base = fixed(part, stage) + (1 - side(bit)) * bit[2]
-        source = sums_ref if stage == 0 else total
 
         def pack(e):
-            block = source[base + spread(e, free), span(part), :]
-            sent[part, start + e] = block.astype(jnp.bfloat16)
+            at = base + spread(e, free)
+            if stage == 0:
+                for k in range(group):
+                    block = tap_block(part, k, at)
+                    sent[part, start + e, pl.ds(k * depth, depth), :] = block.astype(jnp.bfloat16)
+            else:
+                sent[part, start + e] = total[at, span(part), :].astype(jnp.bfloat16)
 
         each(count, pack)
         copy = pltpu.make_async_remote_copy(
@@ -139,12 +153,18 @@
         free = orders[part][stage + 1 :]
         count, start = 1 << len(free), start_of(stage)
         base = fixed(part, stage + 1)
-        source = sums_ref if stage == 0 else total
 
         def step(e):
             at = base + spread(e, free)
-            got = landed[part, start + e].astype(jnp.float32)
-            total[at, span(part), :] = source[at, span(part), :] + got
+            if stage == 0:
+                for k in range(group):
+                    here = pl.ds(k * depth, depth)
+                    got = landed[part, start + e, here, :].astype(jnp.float32)
+                    mine = pl.ds(part * rows + k * depth, depth)
+                    total[at, mine, :] = tap_block(part, k, at) + got
+            else:
+                got = landed[part, start + e].astype(jnp.float32)
+                total[at, span(part), :] = total[at, span(part), :] + got
 
         each(count, step)
 
@@ -160,23 +180,59 @@
                 out_ref[span(part), :] = total[fixed(part, stages), span(part), :]
 
 
-def scatter_sums(sums):
+def exchange(keep, send, axis, step):
+    count = lax.axis_size(axis)
+    got = lax.ppermute(send.astype(jnp.bfloat16), axis, [(i, i ^ step) for i in range(count)])
+    return keep + got.astype(jnp.float32)
+
+
+def halve_chunks(sums, axis, step):
+    taps, chunks, rows, width = sums.shape
+    pairs = sums.reshape(taps, chunks // 2, 2, rows, width)
+    mine = lax.rem(lax.axis_index(axis) // step, 2)
+    keep = lax.dynamic_index_in_dim(pairs, mine, 2, keepdims=False)
+    send = lax.dynamic_index_in_dim(pairs, 1 - mine, 2, keepdims=False)
+    return exchange(keep, send, axis, step)
+
+
+def halve_width(sums, axis, step):
+    half = sums.shape[3] // 2
+    mine = lax.rem(lax.axis_index(axis) // step, 2)
+    low, high = sums[..., :half], sums[..., half:]
+    keep = jnp.where(mine == 0, low, high)
+    send = jnp.where(mine == 0, high, low)
+    return exchange(keep, send, axis, step)
+
+
+def scatter_by_permutes(sums):
     bands, groups = lax.axis_size("space"), lax.axis_size("tm")
     taps, rows, width = sums.shape
+    sums = sums.reshape(taps, bands, rows // bands, width)
+    sums = halve_chunks(sums, "space", 1)
+    step = groups // 2
+    while step >= 1:
+        sums = halve_width(sums, "tm", step)
+        step //= 2
+    step = 2
+    while step < bands:
+        sums = halve_chunks(sums, "space", step)
+        step *= 2
+    return jnp.transpose(sums[:, 0], (0, 2, 1))
+
+
+def scatter_sums(terms):
+    bands, groups = lax.axis_size("space"), lax.axis_size("tm")
+    taps, (rows, width) = len(terms), terms[0].shape
     depth, lanes = rows // bands, width // groups
-    size = taps * depth * lanes
-    blocks = sums.reshape(taps, bands, depth, groups, lanes).transpose(1, 3, 0, 2, 4)
-    blocks = blocks.reshape(bands * groups, size // 128, 128)
-    lines = -(-size // 128 // 16) * 16
-    blocks = jnp.pad(blocks, ((0, 0), (0, lines - size // 128), (0, 0)))
+    if depth % 16 or lanes != 128 or taps % 3:
+        return scatter_by_permutes(jnp.stack(terms))
     orders = bit_orders(bands, groups)
-    if lines % 48:
-        orders = orders[:1]
     parts, stages, devices = len(orders), len(orders[0]), bands * groups
+    lines = taps * depth
     owned = pl.pallas_call(
-        functools.partial(scatter_kernel, orders),
+        functools.partial(scatter_kernel, orders, depth, lanes),
         out_shape=jax.ShapeDtypeStruct((lines, 128), jnp.float32),
-        in_specs=[pl.BlockSpec(memory_space=pltpu.VMEM)],
+        in_specs=[pl.BlockSpec(memory_space=pltpu.VMEM)] * taps,
         out_specs=pl.BlockSpec(memory_space=pltpu.VMEM),
         scratch_shapes=[
             pltpu.VMEM((devices, lines, 128), jnp.float32),
@@ -186,11 +242,10 @@
             pltpu.SemaphoreType.DMA((parts, stages)),
         ],
         compiler_params=pltpu.CompilerParams(
-            collective_id=0, has_side_effects=True, vmem_limit_bytes=24 * 1024 * 1024
+            collective_id=0, has_side_effects=True, vmem_limit_bytes=16 * 1024 * 1024
         ),
-    )(blocks)
-    owned = owned[: size // 128].reshape(taps, depth, lanes)
-    return jnp.transpose(owned, (0, 2, 1))
+    )(*terms)
+    return jnp.transpose(owned.reshape(taps, depth, lanes), (0, 2, 1))
 
 
 def body(frames_in, w_space, w_time, grad_out):
@@ -228,7 +283,7 @@
     block_out, time_terms = temporal_forward(
         jnp.concatenate([past, hidden], axis=0), grad_out, w_time
     )
-    owned = scatter_sums(jnp.stack(terms + time_terms))
+    owned = scatter_sums(terms + time_terms)
     back = jnp.zeros((count * height * width, chans), jnp.float32)
     for i in range(3):
         for j in range(3):

time: 144 us -> 110 us (0.76)
  local copies, waits for them, and re-layouts: 64.7 us -> 32.8 us
  matrix products: 30.4 us -> 25.9 us
  waiting for transfers between devices: 0.02 us -> 2.69 us
  starting transfers between devices: 16.5 us -> 14.7 us
  other arithmetic: 5.28 us -> 7.08 us
    dot_general x13 -> x0, local copies, waits for them, and re-layouts: 18.2 us -> none  [the longest x10 17.1 us: body(): lax.dot_general(flat_pre, source, (((0,), (0,)), ((), ())), preferred_ele...]
    unnamed x91 -> x46, local copies, waits for them, and re-layouts: 16.6 us -> 7.83 us
    dot_general x9, matrix products: 9.42 us -> 2.83 us  [body(): lax.dot_general(flat_pre, source, (((0,), (0,)), ((), ())), preferred_ele...]
    dot_general x3, matrix products: 0.9 us -> 4.14 us  [temporal_forward(): lax.dot_general(flat_grad, source, (((0,), (0,)), ((), ())), preferred_el...]
    ppermute x1, waiting for transfers between devices: 0.01 us -> 2.32 us  [body(): grad_next = lax.ppermute(grad_out[:2], 'tm', [(t, s) for s, t in onward])]
    transpose x1 -> x0, local copies, waits for them, and re-layouts: 2.3 us -> none  [scatter_sums(): sums.reshape(taps, bands, depth, groups, lanes).transpose(1, 3, 0, 2, 4)]
    dot_general x9, matrix products: 4.77 us -> 2.66 us  [body(): jnp.dot(window, w_space[3 * i + j], preferred_element_type=jnp.float32)]
    another operation x4 -> x0, local copies, waits for them, and re-layouts: 2.07 us -> none  [body(): owned = scatter_sums(jnp.stack(terms + time_terms))]
  transfers between devices with their start and end apart: 6 -> 6, of which waited for: 0 -> 2; matrix products, arithmetic and copies ran while one was open for 54% -> 36% of each run, Pallas kernels for 0% -> 0%
where the time goes in v3:
time: 110 us; the launch traced here: 109 us
  local copies, waits for them, and re-layouts  32.8 us (30%)
  matrix products  25.9 us (24%)
  Pallas kernels  24.8 us (23%)
  starting transfers between devices  14.7 us (13%)
  other arithmetic  7.08 us (6%)
  waiting for transfers between devices  2.69 us (2%)
  between operations  1.13 us (1%)
    pallas_call x1, Pallas kernels, scatter_sums(): pl.pallas_call(functools.partial(scatter_kernel, orders, depth, lanes), o...  24.8 us
    slice x9, local copies, waits for them, and re-layouts, body(): grad_ext_rows[:, 2 - i:2 - i + height, 2 - j:2 - j + width]  18.1 us
    dot_general x9, matrix products, body(): lax.dot_general(window, w_space[3 * i + j], (((1,), (1,)), ((), ())), pre...  8.47 us
    unnamed x46, local copies, waits for them, and re-layouts  7.83 us
    ppermute x2, starting transfers between devices, extended_2(): lax.ppermute(lax.slice_in_dim(block, block.shape[dim] - width, None, axis...  6.41 us
    ppermute x1, starting transfers between devices, body(): past = lax.ppermute(hidden[count - 2:], 'tm', onward)  4.39 us
    dot_general x3, matrix products, temporal_forward(): lax.dot_general(flat_grad, source, (((0,), (0,)), ((), ())), preferred_el...  4.14 us
    dot_general x3, matrix products, temporal_backward(): lax.dot_general(later, w_time[k], (((1,), (1,)), ((), ())), preferred_ele...  4.07 us
  transfers between devices with their start and end apart: 6, of which 2 were waited for; matrix products, arithmetic and copies ran while one was open for 36% of the time, Pallas kernels for 0%

profile of v3, /device:TPU:0, one launch (start us, length us, event | category | flops | bytes accessed | tf_op | source)
XLA Modules:
  0.0 109.0 jit_solution(1675876302451007858)
XLA Ops:
  1.7 2.4 %collective-permute-start = (bf16[2,1,128,256]{3,2,1,0:T(8,128)(2,1)S(1)}, bf16[2,1,128,256]{3,2,1,0:T(8,128)(2,1)S(1)}, u32[]{:S(2)}, u32[]{:S(2)}) collective-permute-start(bf16[2,1,128,256]{3,2,1,0:T(8,128)(2,1)S(1)} %get-tuple-element.24), channel_id=1, source_target_pairs={{0,1},{1,2},{2,3},{3,4},{4,5},{5,6},{6,7},{7,8},{8,9},{9,10},{10,1... | collective-permute-start | bytes 393224 | tf_op jit(solution)/shard_map/ppermute | solution.py:16
  4.1 1.3 %collective-permute-start.1 = (bf16[2,1,128,256]{3,2,1,0:T(8,128)(2,1)S(1)}, bf16[2,1,128,256]{3,2,1,0:T(8,128)(2,1)S(1)}, u32[]{:S(2)}, u32[]{:S(2)}) collective-permute-start(bf16[2,1,128,256]{3,2,1,0:T(8,128)(2,1)S(1)} %get-tuple-element.25), channel_id=1, source_target_pairs={{1,0},{2,1},{3,2},{4,3},{5,4},{6,5},{7,6},{8,7},{9,8},{10,9},{11,1... | collective-permute-start | bytes 393224 | tf_op jit(solution)/shard_map/ppermute | solution.py:19
  5.4 1.3 %collective-permute-start.3 = (bf16[2,4,128,256]{3,2,1,0:T(8,128)(2,1)}, bf16[2,4,128,256]{3,2,1,0:T(8,128)(2,1)}, u32[]{:S(2)}, u32[]{:S(2)}) collective-permute-start(bf16[2,4,128,256]{3,2,1,0:T(8,128)(2,1)} %param.7), channel_id=1, source_target_pairs={{16,0},{17,1},{18,2},{19,3},{20,4},{21,5},{22,6},{23,7},{24,8},{25... | collective-permute-start | bytes 1572872 | tf_op jit(solution)/shard_map/ppermute | solution.py:255
  6.7 2.4 %fusion.24 = f32[1024,256]{1,0:T(8,128)} fusion(bf16[1024,256]{1,0:T(8,128)(2,1)} %bitcast.178, bf16[3,256,256]{2,1,0:T(8,128)(2,1)} %param.6), kind=kOutput, calls=%fused_computation.68 | convolution fusion | flops 134217728 | bytes 1703936 | tf_op jit(solution)/shard_map/dot_general | solution.py:49
  10.0 1.2 %copy-done.8 = bf16[9,256,256]{2,1,0:T(8,128)(2,1)S(1)} copy-done((bf16[9,256,256]{2,1,0:T(8,128)(2,1)S(1)}, bf16[9,256,256]{2,1,0:T(8,128)(2,1)}, u32[]{:S(2)}) %copy-start.8) | copy-done | bytes 1179672
  14.0 1.3 %copy.16 = f32[2,4,128,256]{2,3,1,0:T(8,128)} copy(f32[2,4,128,256]{3,2,1,0:T(8,128)S(1)} %bitcast.182) | data formatting | bytes 2097152 | tf_op jit(solution)/shard_map/reshape | solution.py:262
  15.4 2.4 %fusion.23 = f32[1024,256]{1,0:T(8,128)} fusion(f32[1024,256]{1,0:T(8,128)S(1)} %fusion.9, bf16[3,256,256]{2,1,0:T(8,128)(2,1)} %param.6), kind=kOutput, calls=%fused_computation.67 | convolution fusion | flops 135528448 | bytes 2228224 | tf_op jit(solution)/shard_map/dot_general | solution.py:35
  17.7 2.3 %collective-permute-done.3 = bf16[2,4,128,256]{3,2,1,0:T(8,128)(2,1)} collective-permute-done((bf16[2,4,128,256]{3,2,1,0:T(8,128)(2,1)}, bf16[2,4,128,256]{3,2,1,0:T(8,128)(2,1)}, u32[]{:S(2)}, u32[]{:S(2)}) %collective-permute-start.3) | collective-permute-done | bytes 524320 | tf_op jit(solution)/shard_map/ppermute | solution.py:255
  22.3 1.4 %fusion.12 = f32[1024,256]{1,0:T(8,128)S(1)} fusion(f32[1024,256]{1,0:T(8,128)S(1)} %copy-done.14, f32[1024,256]{1,0:T(8,128)S(1)} %fusion.27, bf16[1024,256]{1,0:T(8,128)(2,1)} %bitcast.25, bf16[3,256,256]{2,1,0:T(8,128)(2,1)S(1)} %copy-done.20), kind=kOutput, calls=%fused_computation.32 | convolution fusion | flops 135266304 | bytes 3801088 | tf_op jit(solution)/shard_map/dot_general | solution.py:49
  24.6 1.4 %copy.19 = f32[2,4,128,256]{2,3,1,0:T(8,128)} copy(f32[2,4,128,256]{3,2,1,0:T(8,128)S(1)} %bitcast.183) | data formatting | bytes 2097152 | tf_op jit(solution)/shard_map/convert_element_type | solution.py:269
  26.0 2.8 %multiply_convert_fusion.1 = (bf16[2,4,128,256]{2,3,1,0:T(8,128)(2,1)S(1)}, bf16[2,4,128,256]{2,3,1,0:T(8,128)(2,1)}) fusion(f32[2,4,128,256]{2,3,1,0:T(8,128)} %copy.16, f32[2,4,128,256]{2,3,1,0:T(8,128)} %copy.19), kind=kLoop, calls=%fused_computation.50 | loop fusion | flops 2883584 | bytes 3145728 | tf_op jit(solution)/shard_map/convert_element_type | solution.py:269
  33.4 4.0 %collective-permute-start.4 = (bf16[2,1,128,256]{2,3,1,0:T(8,128)(2,1)S(1)}, bf16[2,1,128,256]{2,3,1,0:T(8,128)(2,1)S(1)}, u32[]{:S(2)}, u32[]{:S(2)}) collective-permute-start(bf16[2,1,128,256]{2,3,1,0:T(8,128)(2,1)S(1)} %get-tuple-element.20), channel_id=1, source_target_pairs={{0,1},{1,2},{2,3},{3,4},{4,5},{5,6},{6,7},{7,8},{8,9},{9,10},{10,1... | collective-permute-start | bytes 393224 | tf_op jit(solution)/shard_map/ppermute | solution.py:16
  37.4 1.3 %collective-permute-start.5 = (bf16[2,1,128,256]{2,3,1,0:T(8,128)(2,1)S(1)}, bf16[2,1,128,256]{2,3,1,0:T(8,128)(2,1)S(1)}, u32[]{:S(2)}, u32[]{:S(2)}) collective-permute-start(bf16[2,1,128,256]{2,3,1,0:T(8,128)(2,1)S(1)} %get-tuple-element.21), channel_id=1, source_target_pairs={{1,0},{2,1},{3,2},{4,3},{5,4},{6,5},{7,6},{8,7},{9,8},{10,9},{11,1... | collective-permute-start | bytes 393224 | tf_op jit(solution)/shard_map/ppermute | solution.py:19
  38.7 4.4 %collective-permute-start.2 = (bf16[2,4,128,256]{2,3,1,0:T(8,128)(2,1)}, bf16[2,4,128,256]{2,3,1,0:T(8,128)(2,1)}, u32[]{:S(2)}, u32[]{:S(2)}) collective-permute-start(bf16[2,4,128,256]{2,3,1,0:T(8,128)(2,1)} %get-tuple-element.11), channel_id=1, source_target_pairs={{0,16},{1,17},{2,18},{3,19},{4,20},{5,21},{6,22},{7,23},{8,24},{9,... | collective-permute-start | bytes 1572872 | tf_op jit(solution)/shard_map/ppermute | solution.py:264
  43.1 1.4 %convolution_bitcast_fusion.refs_11_ = f32[256,256]{1,0:T(8,128)S(1)} fusion(bf16[2,4,128,256]{2,3,1,0:T(8,128)(2,1)} %get-tuple-element.11, bf16[2,4,128,256]{3,2,1,0:T(8,128)(2,1)S(1)} %copy-done.3), kind=kOutput, calls=%fused_computation.34 | convolution fusion | flops 134217728 | bytes 1310720 | tf_op jit(solution)/shard_map/dot_general | solution.py:37
  45.6 2.1 %copy.27 = bf16[2,4,128,256]{3,2,1,0:T(8,128)(2,1)} copy(bf16[2,4,128,256]{2,3,1,0:T(8,128)(2,1)} %get-tuple-element.18) | data formatting | bytes 1048576 | tf_op jit(solution)/shard_map/slice | solution.py:290
  47.7 2.0 %copy.22 = bf16[2,4,128,256]{3,2,1,0:T(8,128)(2,1)} copy(bf16[2,4,128,256]{2,3,1,0:T(8,128)(2,1)} %get-tuple-element.19) | data formatting | bytes 1048576 | tf_op jit(solution)/shard_map/slice | solution.py:290
  49.7 2.4 %fusion.48 = f32[1024,256]{1,0:T(8,128)} fusion(bf16[1024,256]{1,0:T(8,128)(2,1)} %bitcast.193, bf16[9,256,256]{2,1,0:T(8,128)(2,1)} %param.5), kind=kOutput, calls=%fused_computation.92 | convolution fusion | flops 134217728 | bytes 1703936 | tf_op jit(solution)/shard_map/dot_general | solution.py:293
  52.9 2.5 %fusion.88 = (bf16[2,4,128,256]{2,3,1,0:T(8,128)(2,1)}, bf16[2,4,128,256]{2,3,1,0:T(8,128)(2,1)}, bf16[2,4,128,256]{2,3,1,0:T(8,128)(2,1)}, bf16[2,4,128,256]{2,...) fusion(bf16[2,6,130,256]{2,3,1,0:T(8,128)(2,1)S(1)} %fusion.6), kind=kLoop, calls=%fused_computation.132 | loop fusion | bytes 6291456 | tf_op jit(solution)/shard_map/slice | solution.py:290
  55.3 1.2 %copy.28 = bf16[2,4,128,256]{3,2,1,0:T(8,128)(2,1)S(1)} copy(bf16[2,4,128,256]{2,3,1,0:T(8,128)(2,1)} %get-tuple-element.4) | data formatting | bytes 1048576 | tf_op jit(solution)/shard_map/slice | solution.py:290
  56.6 2.0 %copy.26 = bf16[2,4,128,256]{3,2,1,0:T(8,128)(2,1)} copy(bf16[2,4,128,256]{2,3,1,0:T(8,128)(2,1)} %get-tuple-element.5) | data formatting | bytes 1048576 | tf_op jit(solution)/shard_map/slice | solution.py:290
  58.6 2.0 %copy.25 = bf16[2,4,128,256]{3,2,1,0:T(8,128)(2,1)} copy(bf16[2,4,128,256]{2,3,1,0:T(8,128)(2,1)} %get-tuple-element.6) | data formatting | bytes 1048576 | tf_op jit(solution)/shard_map/slice | solution.py:290
  60.7 2.1 %copy.24 = bf16[2,4,128,256]{3,2,1,0:T(8,128)(2,1)} copy(bf16[2,4,128,256]{2,3,1,0:T(8,128)(2,1)} %get-tuple-element.7) | data formatting | bytes 1048576 | tf_op jit(solution)/shard_map/slice | solution.py:290
  62.8 2.0 %copy.23 = bf16[2,4,128,256]{3,2,1,0:T(8,128)(2,1)} copy(bf16[2,4,128,256]{2,3,1,0:T(8,128)(2,1)} %get-tuple-element.8) | data formatting | bytes 1048576 | tf_op jit(solution)/shard_map/slice | solution.py:290
  64.8 2.0 %copy.21 = bf16[2,4,128,256]{3,2,1,0:T(8,128)(2,1)} copy(bf16[2,4,128,256]{2,3,1,0:T(8,128)(2,1)} %get-tuple-element.9) | data formatting | bytes 1048576 | tf_op jit(solution)/shard_map/slice | solution.py:290
  66.8 1.5 %fusion.51 = f32[1024,256]{1,0:T(8,128)S(1)} fusion(bf16[1024,256]{1,0:T(8,128)(2,1)} %bitcast.194, bf16[9,256,256]{2,1,0:T(8,128)(2,1)} %param.5), kind=kOutput, calls=%fused_computation.95 | convolution fusion | flops 134217728 | bytes 1703936 | tf_op jit(solution)/shard_map/dot_general | solution.py:293
  68.4 1.6 %convolution_add_fusion.6 = f32[1024,256]{1,0:T(8,128)S(1)} fusion(bf16[1024,256]{1,0:T(8,128)(2,1)S(1)} %bitcast.200, f32[1024,256]{1,0:T(8,128)S(1)} %fusion.51, f32[1024,256]{1,0:T(8,128)} %fusion.48, bf16[9,256,256]{2,1,0:T(8,128)(2,1)S(1)} %copy-done.9), kind=kOutput, calls=%fused_computation.17 | convolution fusion | flops 134742016 | bytes 3801088 | tf_op jit(solution)/shard_map/dot_general | solution.py:293
  76.2 1.4 %convolution_bitcast_fusion.1.refs_9_ = f32[256,256]{1,0:T(8,128)S(1)} fusion(bf16[2,4,128,256]{2,3,1,0:T(8,128)(2,1)} %collective-permute-done.2, bf16[2,4,128,256]{3,2,1,0:T(8,128)(2,1)S(1)} %copy-done.4), kind=kOutput, calls=%fused_computation.35 | convolution fusion | flops 134217728 | bytes 1310720 | tf_op jit(solution)/shard_map/dot_general | solution.py:37
  77.6 1.4 %convolution_bitcast_fusion.11.refs_10_ = f32[256,256]{1,0:T(8,128)S(1)} fusion(bf16[2,4,128,256]{3,2,1,0:T(8,128)(2,1)S(1)} %copy-done.4, bf16[2,4,128,256]{2,3,1,0:T(8,128)(2,1)} %get-tuple-element.11, bf16[2,4,128,256]{2,3,1,0:T(8,128)(2,1)} %collective-permute-done.2), kind=kOutput, calls=%fused_computation.45 | convolution fusion | flops 136314880 | bytes 1835008 | tf_op jit(solution)/shard_map/dot_general | solution.py:37
  79.0 24.8 %shard_map.75 = f32[192,128]{1,0:T(8,128)S(1)} custom-call(f32[256,256]{1,0:T(8,128)S(1)} %convolution_bitcast_fusion.10.refs_0_, f32[256,256]{1,0:T(8,128)S(1)} %convolution_bitcast_fusion.9.refs_1_, f32[256,256]{1,0:T(8,128)S(1)} %convolution_bitcast_fusion.8.refs_2_, f32[256,256]{1,0:T(8,128)S(1)} %convolution_bitcast_fusion.7.refs_3_, ...), custom_call_target="tpu_custom_call" | custom-call | tf_op jit(solution)/shard_map/pallas_call | solution.py:232
  105.0 1.1 %pad_maximum_fusion.3 = bf16[2,4,128,256]{2,3,1,0:T(8,128)(2,1)S(1)} fusion(bf16[2,4,128,256]{2,3,1,0:T(8,128)(2,1)} %get-tuple-element.11, bf16[2,4,128,256]{2,3,1,0:T(8,128)(2,1)} %collective-permute-done.2), kind=kLoop, calls=%fused_computation.63 | loop fusion | flops 262144 | bytes 1572864 | tf_op jit(solution)/shard_map/slice | solution.py:34
  106.6 1.3 %copy.17 = bf16[2,4,128,256]{3,2,1,0:T(8,128)(2,1)S(1)} copy(bf16[2,4,128,256]{2,3,1,0:T(8,128)(2,1)} %collective-permute-done.2) | data formatting | bytes 1048576 | tf_op jit(solution)/shard_map/ppermute | solution.py:264
  (88 shorter events, 23.2 us)
Async XLA Ops:
  0.6 8.8 %copy-start.5 = (bf16[2,4,128,256]{3,2,1,0:T(8,128)(2,1)S(1)}, bf16[2,4,128,256]{3,2,1,0:T(8,128)(2,1)}, u32[]{:S(2)}) copy-start(bf16[2,4,128,256]{3,2,1,0:T(8,128)(2,1)} %param.4) | copy-start | bytes 1572868
  1.7 7.4 %collective-permute-start = (bf16[2,1,128,256]{3,2,1,0:T(8,128)(2,1)S(1)}, bf16[2,1,128,256]{3,2,1,0:T(8,128)(2,1)S(1)}, u32[]{:S(2)}, u32[]{:S(2)}) collective-permute-start(bf16[2,1,128,256]{3,2,1,0:T(8,128)(2,1)S(1)} %get-tuple-element.24), channel_id=1, source_target_pairs={{0,1},{1,2},{2,3},{3,4},{4,5},{5,6},{6,7},{7,8},{8,9},{9,10},{10,1... | collective-permute-start | bytes 393224 | tf_op jit(solution)/shard_map/ppermute | solution.py:16
  4.1 5.3 %collective-permute-start.1 = (bf16[2,1,128,256]{3,2,1,0:T(8,128)(2,1)S(1)}, bf16[2,1,128,256]{3,2,1,0:T(8,128)(2,1)S(1)}, u32[]{:S(2)}, u32[]{:S(2)}) collective-permute-start(bf16[2,1,128,256]{3,2,1,0:T(8,128)(2,1)S(1)} %get-tuple-element.25), channel_id=1, source_target_pairs={{1,0},{2,1},{3,2},{4,3},{5,4},{6,5},{7,6},{8,7},{9,8},{10,9},{11,1... | collective-permute-start | bytes 393224 | tf_op jit(solution)/shard_map/ppermute | solution.py:19
  5.4 14.7 %collective-permute-start.3 = (bf16[2,4,128,256]{3,2,1,0:T(8,128)(2,1)}, bf16[2,4,128,256]{3,2,1,0:T(8,128)(2,1)}, u32[]{:S(2)}, u32[]{:S(2)}) collective-permute-start(bf16[2,4,128,256]{3,2,1,0:T(8,128)(2,1)} %param.7), channel_id=1, source_target_pairs={{16,0},{17,1},{18,2},{19,3},{20,4},{21,5},{22,6},{23,7},{24,8},{25... | collective-permute-start | bytes 1572872 | tf_op jit(solution)/shard_map/ppermute | solution.py:255
  9.6 20.9 %copy-start = (bf16[2,6,130,256]{3,2,1,0:T(8,128)(2,1)}, bf16[2,6,130,256]{3,2,1,0:T(8,128)(2,1)S(1)}, u32[]{:S(2)}) copy-start(bf16[2,6,130,256]{3,2,1,0:T(8,128)(2,1)S(1)} %fusion.21) | copy-start | bytes 2396164
  9.6 1.6 %copy-start.8 = (bf16[9,256,256]{2,1,0:T(8,128)(2,1)S(1)}, bf16[9,256,256]{2,1,0:T(8,128)(2,1)}, u32[]{:S(2)}) copy-start(bf16[9,256,256]{2,1,0:T(8,128)(2,1)} %param.5) | copy-start | bytes 3538948
  11.9 1.8 %copy-start.6 = (bf16[2,4,128,256]{3,2,1,0:T(8,128)(2,1)}, bf16[2,4,128,256]{3,2,1,0:T(8,128)(2,1)S(1)}, u32[]{:S(2)}) copy-start(bf16[2,4,128,256]{3,2,1,0:T(8,128)(2,1)S(1)} %get-tuple-element.22) | copy-start | bytes 1572868
  14.0 3.7 %copy-start.10 = (f32[1024,256]{1,0:T(8,128)}, f32[1024,256]{1,0:T(8,128)S(1)}, u32[]{:S(2)}) copy-start(f32[1024,256]{1,0:T(8,128)S(1)} %fusion.9) | copy-start | bytes 3145732
  15.4 4.7 %copy-start.2 = (bf16[2,4,128,256]{3,2,1,0:T(8,128)(2,1)S(1)}, bf16[2,4,128,256]{3,2,1,0:T(8,128)(2,1)}, u32[]{:S(2)}) copy-start(bf16[2,4,128,256]{3,2,1,0:T(8,128)(2,1)} %param.7) | copy-start | bytes 1572868
  17.7 3.3 %copy-start.20 = (bf16[3,256,256]{2,1,0:T(8,128)(2,1)S(1)}, bf16[3,256,256]{2,1,0:T(8,128)(2,1)}, u32[]{:S(2)}) copy-start(bf16[3,256,256]{2,1,0:T(8,128)(2,1)} %param.6) | copy-start | bytes 1179652
  21.1 1.2 %copy-start.14 = (f32[1024,256]{1,0:T(8,128)S(1)}, f32[1024,256]{1,0:T(8,128)}, u32[]{:S(2)}) copy-start(f32[1024,256]{1,0:T(8,128)} %fusion.24) | copy-start | bytes 3145732
  23.7 1.0 copy-start.12
  28.9 1.0 copy-start.7
  30.9 1.2 %copy-start.1 = (bf16[2,6,130,256]{3,2,1,0:T(8,128)(2,1)S(1)}, bf16[2,6,130,256]{3,2,1,0:T(8,128)(2,1)}, u32[]{:S(2)}) copy-start(bf16[2,6,130,256]{3,2,1,0:T(8,128)(2,1)} %copy-done) | copy-start | bytes 2396164
  33.0 10.1 %copy-start.3 = (bf16[2,4,128,256]{3,2,1,0:T(8,128)(2,1)S(1)}, bf16[2,4,128,256]{3,2,1,0:T(8,128)(2,1)}, u32[]{:S(2)}) copy-start(bf16[2,4,128,256]{3,2,1,0:T(8,128)(2,1)} %param.7) | copy-start | bytes 1572868
  33.4 11.1 %collective-permute-start.4 = (bf16[2,1,128,256]{2,3,1,0:T(8,128)(2,1)S(1)}, bf16[2,1,128,256]{2,3,1,0:T(8,128)(2,1)S(1)}, u32[]{:S(2)}, u32[]{:S(2)}) collective-permute-start(bf16[2,1,128,256]{2,3,1,0:T(8,128)(2,1)S(1)} %get-tuple-element.20), channel_id=1, source_target_pairs={{0,1},{1,2},{2,3},{3,4},{4,5},{5,6},{6,7},{7,8},{8,9},{9,10},{10,1... | collective-permute-start | bytes 393224 | tf_op jit(solution)/shard_map/ppermute | solution.py:16
  37.4 7.1 %collective-permute-start.5 = (bf16[2,1,128,256]{2,3,1,0:T(8,128)(2,1)S(1)}, bf16[2,1,128,256]{2,3,1,0:T(8,128)(2,1)S(1)}, u32[]{:S(2)}, u32[]{:S(2)}) collective-permute-start(bf16[2,1,128,256]{2,3,1,0:T(8,128)(2,1)S(1)} %get-tuple-element.21), channel_id=1, source_target_pairs={{1,0},{2,1},{3,2},{4,3},{5,4},{6,5},{7,6},{8,7},{9,8},{10,9},{11,1... | collective-permute-start | bytes 393224 | tf_op jit(solution)/shard_map/ppermute | solution.py:19
  38.7 37.4 %collective-permute-start.2 = (bf16[2,4,128,256]{2,3,1,0:T(8,128)(2,1)}, bf16[2,4,128,256]{2,3,1,0:T(8,128)(2,1)}, u32[]{:S(2)}, u32[]{:S(2)}) collective-permute-start(bf16[2,4,128,256]{2,3,1,0:T(8,128)(2,1)} %get-tuple-element.11), channel_id=1, source_target_pairs={{0,16},{1,17},{2,18},{3,19},{4,20},{5,21},{6,22},{7,23},{8,24},{9,... | collective-permute-start | bytes 1572872 | tf_op jit(solution)/shard_map/ppermute | solution.py:264
  66.8 1.5 %copy-start.9 = (bf16[9,256,256]{2,1,0:T(8,128)(2,1)S(1)}, bf16[9,256,256]{2,1,0:T(8,128)(2,1)}, u32[]{:S(2)}) copy-start(bf16[9,256,256]{2,1,0:T(8,128)(2,1)} %param.5) | copy-start | bytes 3538948
  66.8 1.6 %copy-start.19 = (bf16[2,4,128,256]{3,2,1,0:T(8,128)(2,1)S(1)}, bf16[2,4,128,256]{3,2,1,0:T(8,128)(2,1)}, u32[]{:S(2)}) copy-start(bf16[2,4,128,256]{3,2,1,0:T(8,128)(2,1)} %copy.23) | copy-start | bytes 1572868
  68.4 1.6 %copy-start.18 = (bf16[2,4,128,256]{3,2,1,0:T(8,128)(2,1)S(1)}, bf16[2,4,128,256]{3,2,1,0:T(8,128)(2,1)}, u32[]{:S(2)}) copy-start(bf16[2,4,128,256]{3,2,1,0:T(8,128)(2,1)} %copy.24) | copy-start | bytes 1572868
  70.0 1.2 %copy-start.11 = (f32[1024,256]{1,0:T(8,128)S(1)}, f32[1024,256]{1,0:T(8,128)}, u32[]{:S(2)}) copy-start(f32[1024,256]{1,0:T(8,128)} %copy-done.10) | copy-start | bytes 3145732
  70.0 1.5 %copy-start.13 = (f32[1024,256]{1,0:T(8,128)S(1)}, f32[1024,256]{1,0:T(8,128)}, u32[]{:S(2)}) copy-start(f32[1024,256]{1,0:T(8,128)} %copy-done.12) | copy-start | bytes 3145732
  71.6 1.0 copy-start.17
  72.6 1.0 copy-start.16
  73.7 1.0 copy-start.15
  75.0 1.1 %copy-start.4 = (bf16[2,4,128,256]{3,2,1,0:T(8,128)(2,1)S(1)}, bf16[2,4,128,256]{3,2,1,0:T(8,128)(2,1)}, u32[]{:S(2)}) copy-start(bf16[2,4,128,256]{3,2,1,0:T(8,128)(2,1)} %param.7) | copy-start | bytes 1572868
  105.0 1.4 %copy-start.21 = (bf16[3,256,256]{2,1,0:T(8,128)(2,1)S(1)}, bf16[3,256,256]{2,1,0:T(8,128)(2,1)}, u32[]{:S(2)}) copy-start(bf16[3,256,256]{2,1,0:T(8,128)(2,1)} %param.6) | copy-start | bytes 1179652
  106.3 1.6 %copy-start.22 = (f32[1024,256]{1,0:T(8,128)S(1)}, f32[1024,256]{1,0:T(8,128)}, u32[]{:S(2)}) copy-start(f32[1024,256]{1,0:T(8,128)} %fusion.23) | copy-start | bytes 3145732

commit v4 on v3

--- a/solution.py
+++ b/solution.py
@@ -4,6 +4,7 @@
 import jax.numpy as jnp
 from jax import lax
 from jax.experimental import pallas as pl
+from jax.experimental.layout import Layout, with_layout_constraint
 from jax.experimental.pallas import tpu as pltpu
 from jax.sharding import PartitionSpec as P
 
@@ -53,6 +54,10 @@
 
 
 MESH = pl.DeviceIdType.MESH
+
+
+def rows_major(field):
+    return with_layout_constraint(field, Layout(tuple(range(field.ndim))))
 
 
 def bit_orders(bands, groups):
@@ -259,8 +264,8 @@
         for j in range(3):
             window = extended[:, i : i + height, j : j + width].reshape(-1, chans)
             pre = pre + jnp.dot(window, w_space[3 * i + j], preferred_element_type=jnp.float32)
-    pre = pre.reshape(count, height, width, chans)
-    hidden = jax.nn.silu(pre).astype(jnp.bfloat16)
+    pre = rows_major(pre.reshape(count, height, width, chans))
+    hidden = rows_major(jax.nn.silu(pre).astype(jnp.bfloat16))
     past = lax.ppermute(hidden[count - 2 :], "tm", onward)
     grad_hidden = temporal_backward(
         jnp.concatenate([grad_out, grad_next], axis=0), w_time, count
@@ -269,7 +274,8 @@
     grad_pre = (grad_hidden.astype(jnp.float32) * sig * (1.0 + pre * (1.0 - sig))).astype(
         jnp.bfloat16
     )
-    grad_ext_rows = pad_columns(extended_2(grad_pre, (("space", 1),), 1))
+    grad_pre = rows_major(grad_pre)
+    grad_ext_rows = rows_major(pad_columns(extended_2(grad_pre, (("space", 1),), 1)))
     flat_pre = grad_pre.reshape(-1, chans)
     terms = []
     for i in range(3):

time: 110 us -> 73.9 us (0.67)
  local copies, waits for them, and re-layouts: 32.8 us -> 4.04 us
  matrix products: 25.9 us -> 14.3 us
  waiting for transfers between devices: 2.69 us -> 11 us
  other arithmetic: 7.08 us -> 1.19 us
  Pallas kernels: 24.8 us -> 29.9 us
  starting transfers between devices: 14.7 us -> 12.2 us
    slice x9 -> x1, local copies, waits for them, and re-layouts: 18.1 us -> 0.45 us  [body(): grad_ext_rows[:, 2 - i:2 - i + height, 2 - j:2 - j + width]]
    unnamed x46 -> x8, local copies, waits for them, and re-layouts: 7.83 us -> 0.83 us
    pallas_call x1, Pallas kernels: 24.8 us -> 29.9 us  [scatter_sums(): pl.pallas_call(functools.partial(scatter_kernel, orders, depth, lanes), o...]
    dot_general x9, matrix products: 8.47 us -> 3.77 us  [body(): lax.dot_general(window, w_space[3 * i + j], (((1,), (1,)), ((), ())), pre...]
    ppermute x2, waiting for transfers between devices: 0.36 us -> 4.31 us  [extended_2(): lax.ppermute(lax.slice_in_dim(block, 0, width, axis=dim), axis, backward)]
    ppermute x1, waiting for transfers between devices: 2.32 us -> 6.19 us  [body(): grad_next = lax.ppermute(grad_out[:2], 'tm', [(t, s) for s, t in onward])]
    dot_general x3, matrix products: 4.14 us -> 1.04 us  [temporal_forward(): lax.dot_general(flat_grad, source, (((0,), (0,)), ((), ())), preferred_el...]
    ppermute x1, starting transfers between devices: 4.39 us -> 1.87 us  [body(): past = lax.ppermute(hidden[count - 2:], 'tm', onward)]
  transfers between devices with their start and end apart: 6 -> 6, of which waited for: 2 -> 4; matrix products, arithmetic and copies ran while one was open for 36% -> 14% of each run, Pallas kernels for 0% -> 0%
where the time goes in v4:
time: 73.9 us; the launch traced here: 73.6 us
  Pallas kernels  29.9 us (40%)
  matrix products  14.3 us (19%)
  starting transfers between devices  12.2 us (17%)
  waiting for transfers between devices  11 us (15%)
  local copies, waits for them, and re-layouts  4.04 us (5%)
  other arithmetic  1.19 us (2%)
  between operations  1 us (1%)
    pallas_call x1, Pallas kernels, scatter_sums(): pl.pallas_call(functools.partial(scatter_kernel, orders, depth, lanes), o...  29.9 us
    ppermute x2, starting transfers between devices, extended_2(): lax.ppermute(lax.slice_in_dim(block, block.shape[dim] - width, None, axis...  6.44 us
    ppermute x1, waiting for transfers between devices, body(): grad_next = lax.ppermute(grad_out[:2], 'tm', [(t, s) for s, t in onward])  6.19 us
    ppermute x2, waiting for transfers between devices, extended_2(): lax.ppermute(lax.slice_in_dim(block, 0, width, axis=dim), axis, backward)  4.31 us
    dot_general x9, matrix products, body(): lax.dot_general(window, w_space[3 * i + j], (((1,), (1,)), ((), ())), pre...  3.77 us
    dot_general x9, matrix products, body(): lax.dot_general(flat_pre, source, (((0,), (0,)), ((), ())), preferred_ele...  3.02 us
    dot_general x9, matrix products, body(): jnp.dot(window, w_space[3 * i + j], preferred_element_type=jnp.float32)  2.68 us
    ppermute x2, starting transfers between devices, extended_2(): lax.ppermute(lax.slice_in_dim(block, 0, width, axis=dim), axis, backward)  2.58 us
  transfers between devices with their start and end apart: 6, of which 4 were waited for; matrix products, arithmetic and copies ran while one was open for 14% of the time, Pallas kernels for 0%

profile of v4, /device:TPU:0, one launch (start us, length us, event | category | flops | bytes accessed | tf_op | source)
XLA Modules:
  0.0 73.6 jit_solution(11342322139380180581)
XLA Ops:
  0.6 1.0 %fusion.80 = (bf16[2,1,128,256]{3,2,1,0:T(8,128)(2,1)S(1)}, bf16[2,1,128,256]{3,2,1,0:T(8,128)(2,1)S(1)}) fusion(bf16[2,4,128,256]{3,2,1,0:T(8,128)(2,1)} %param.4), kind=kLoop, calls=%fused_computation.123 | loop fusion | bytes 524288 | tf_op jit(solution)/shard_map/slice | solution.py:18
  1.7 2.4 %collective-permute-start = (bf16[2,1,128,256]{3,2,1,0:T(8,128)(2,1)S(1)}, bf16[2,1,128,256]{3,2,1,0:T(8,128)(2,1)S(1)}, u32[]{:S(2)}, u32[]{:S(2)}) collective-permute-start(bf16[2,1,128,256]{3,2,1,0:T(8,128)(2,1)S(1)} %get-tuple-element.24), channel_id=1, source_target_pairs={{0,1},{1,2},{2,3},{3,4},{4,5},{5,6},{6,7},{7,8},{8,9},{9,10},{10,1... | collective-permute-start | bytes 393224 | tf_op jit(solution)/shard_map/ppermute | solution.py:17
  4.1 1.3 %collective-permute-start.1 = (bf16[2,1,128,256]{3,2,1,0:T(8,128)(2,1)S(1)}, bf16[2,1,128,256]{3,2,1,0:T(8,128)(2,1)S(1)}, u32[]{:S(2)}, u32[]{:S(2)}) collective-permute-start(bf16[2,1,128,256]{3,2,1,0:T(8,128)(2,1)S(1)} %get-tuple-element.25), channel_id=1, source_target_pairs={{1,0},{2,1},{3,2},{4,3},{5,4},{6,5},{7,6},{8,7},{9,8},{10,9},{11,1... | collective-permute-start | bytes 393224 | tf_op jit(solution)/shard_map/ppermute | solution.py:20
  5.4 1.3 %collective-permute-start.3 = (bf16[2,4,128,256]{3,2,1,0:T(8,128)(2,1)}, bf16[2,4,128,256]{3,2,1,0:T(8,128)(2,1)S(1)}, u32[]{:S(2)}, u32[]{:S(2)}) collective-permute-start(bf16[2,4,128,256]{3,2,1,0:T(8,128)(2,1)} %param.7), channel_id=1, source_target_pairs={{16,0},{17,1},{18,2},{19,3},{20,4},{21,5},{22,6},{23,7},{24,8},{25... | collective-permute-start | bytes 1572872 | tf_op jit(solution)/shard_map/ppermute | solution.py:260
  6.7 1.4 %fusion.14 = f32[1024,256]{1,0:T(8,128)S(1)} fusion(bf16[1024,256]{1,0:T(8,128)(2,1)} %bitcast.185, bf16[3,256,256]{2,1,0:T(8,128)(2,1)} %param.6), kind=kOutput, calls=%fused_computation.57 | convolution fusion | flops 134217728 | bytes 1703936 | tf_op jit(solution)/shard_map/dot_general | solution.py:50
  8.1 1.3 %collective-permute-done.1 = bf16[2,1,128,256]{3,2,1,0:T(8,128)(2,1)S(1)} collective-permute-done((bf16[2,1,128,256]{3,2,1,0:T(8,128)(2,1)S(1)}, bf16[2,1,128,256]{3,2,1,0:T(8,128)(2,1)S(1)}, u32[]{:S(2)}, u32[]{:S(2)}) %collective-permute-start.1) | collective-permute-done | bytes 131104 | tf_op jit(solution)/shard_map/ppermute | solution.py:20
  9.6 0.4 fusion.78
  10.1 0.8 %copy-done.2 = bf16[9,256,256]{2,1,0:T(8,128)(2,1)S(1)} copy-done((bf16[9,256,256]{2,1,0:T(8,128)(2,1)S(1)}, bf16[9,256,256]{2,1,0:T(8,128)(2,1)}, u32[]{:S(2)}) %copy-start.2) | copy-done | bytes 1179672
  13.7 6.2 %collective-permute-done.3 = bf16[2,4,128,256]{3,2,1,0:T(8,128)(2,1)S(1)} collective-permute-done((bf16[2,4,128,256]{3,2,1,0:T(8,128)(2,1)}, bf16[2,4,128,256]{3,2,1,0:T(8,128)(2,1)S(1)}, u32[]{:S(2)}, u32[]{:S(2)}) %collective-permute-start.3) | collective-permute-done | bytes 524320 | tf_op jit(solution)/shard_map/ppermute | solution.py:260
  20.3 0.4 fusion.6
  20.7 0.5 fusion.12
  21.2 0.3 convolution_bitcast_fusion.3.refs_7_
  21.6 0.3 convolution_bitcast_fusion.9.refs_1_
  22.2 0.3 convolution_bitcast_fusion.5.refs_5_
  22.6 0.3 convolution_bitcast_fusion.6.refs_4_
  22.9 0.3 convolution_bitcast_fusion.7.refs_3_
  23.3 0.3 convolution_bitcast_fusion.8.refs_2_
  23.9 0.3 convolution_bitcast_fusion.2.refs_8_
  24.3 4.1 %collective-permute-start.4 = (bf16[2,1,128,256]{3,2,1,0:T(8,128)(2,1)S(1)}, bf16[2,1,128,256]{3,2,1,0:T(8,128)(2,1)S(1)}, u32[]{:S(2)}, u32[]{:S(2)}) collective-permute-start(bf16[2,1,128,256]{3,2,1,0:T(8,128)(2,1)S(1)} %get-tuple-element.20), channel_id=1, source_target_pairs={{0,1},{1,2},{2,3},{3,4},{4,5},{5,6},{6,7},{7,8},{8,9},{9,10},{10,1... | collective-permute-start | bytes 393224 | tf_op jit(solution)/shard_map/ppermute | solution.py:17
  28.4 1.3 %collective-permute-start.5 = (bf16[2,1,128,256]{3,2,1,0:T(8,128)(2,1)S(1)}, bf16[2,1,128,256]{3,2,1,0:T(8,128)(2,1)S(1)}, u32[]{:S(2)}, u32[]{:S(2)}) collective-permute-start(bf16[2,1,128,256]{3,2,1,0:T(8,128)(2,1)S(1)} %get-tuple-element.21), channel_id=1, source_target_pairs={{1,0},{2,1},{3,2},{4,3},{5,4},{6,5},{7,6},{8,7},{9,8},{10,9},{11,1... | collective-permute-start | bytes 393224 | tf_op jit(solution)/shard_map/ppermute | solution.py:20
  29.7 1.9 %collective-permute-start.2 = (bf16[2,4,128,256]{3,2,1,0:T(8,128)(2,1)S(1)}, bf16[2,4,128,256]{3,2,1,0:T(8,128)(2,1)S(1)}, u32[]{:S(2)}, u32[]{:S(2)}) collective-permute-start(bf16[2,4,128,256]{3,2,1,0:T(8,128)(2,1)S(1)} %get-tuple-element.5), channel_id=1, source_target_pairs={{0,16},{1,17},{2,18},{3,19},{4,20},{5,21},{6,22},{7,23},{8,24},{9,... | collective-permute-start | bytes 1572872 | tf_op jit(solution)/shard_map/ppermute | solution.py:269
  31.9 0.4 convolution_bitcast_fusion.refs_11_
  32.3 3.0 %collective-permute-done.5 = bf16[2,1,128,256]{3,2,1,0:T(8,128)(2,1)S(1)} collective-permute-done((bf16[2,1,128,256]{3,2,1,0:T(8,128)(2,1)S(1)}, bf16[2,1,128,256]{3,2,1,0:T(8,128)(2,1)S(1)}, u32[]{:S(2)}, u32[]{:S(2)}) %collective-permute-start.5) | collective-permute-done | bytes 131104 | tf_op jit(solution)/shard_map/ppermute | solution.py:20
  35.5 0.4 fusion.77
  38.7 1.1 %fusion.7 = bf16[1024,256]{1,0:T(8,128)(2,1)} fusion(f32[1024,256]{1,0:T(8,128)S(1)} %fusion.24, f32[1024,256]{1,0:T(8,128)S(1)} %convolution_add_fusion.1, bf16[1024,256]{1,0:T(8,128)(2,1)S(1)} %bitcast.192, bf16[9,256,256]{2,1,0:T(8,128)(2,1)S(1)} %copy-done.2), kind=kOutput, calls=%fused_computation.25 | convolution fusion | flops 135004160 | bytes 3276800 | tf_op jit(solution)/shard_map/dot_general | solution.py:299
  39.8 0.5 collective-permute-done.2
  40.3 0.3 convolution_bitcast_fusion.1.refs_9_
  40.7 0.3 convolution_bitcast_fusion.11.refs_10_
  41.0 29.9 %shard_map.75 = f32[192,128]{1,0:T(8,128)S(1)} custom-call(f32[256,256]{1,0:T(8,128)S(1)} %convolution_bitcast_fusion.10.refs_0_, f32[256,256]{1,0:T(8,128)S(1)} %convolution_bitcast_fusion.9.refs_1_, f32[256,256]{1,0:T(8,128)S(1)} %convolution_bitcast_fusion.8.refs_2_, f32[256,256]{1,0:T(8,128)S(1)} %convolution_bitcast_fusion.7.refs_3_, ...), custom_call_target="tpu_custom_call" | custom-call | tf_op jit(solution)/shard_map/pallas_call | solution.py:237
  70.9 0.6 slice.195
  71.5 0.6 slice.194
  72.5 1.1 %fusion.5 = bf16[1024,256]{1,0:T(8,128)(2,1)} fusion(f32[1024,256]{1,0:T(8,128)S(1)} %fusion.16, f32[1024,256]{1,0:T(8,128)S(1)} %fusion.20, bf16[1024,256]{1,0:T(8,128)(2,1)S(1)} %bitcast.187, bf16[3,256,256]{2,1,0:T(8,128)(2,1)S(1)} %copy-done.3), kind=kOutput, calls=%fused_computation.23 | convolution fusion | flops 135004160 | bytes 3276800 | tf_op jit(solution)/shard_map/dot_general | solution.py:36
  (38 shorter events, 7.6 us)
Async XLA Ops:
  0.6 8.8 %copy-start.1 = (bf16[2,4,128,256]{3,2,1,0:T(8,128)(2,1)S(1)}, bf16[2,4,128,256]{3,2,1,0:T(8,128)(2,1)}, u32[]{:S(2)}) copy-start(bf16[2,4,128,256]{3,2,1,0:T(8,128)(2,1)} %param.4) | copy-start | bytes 1572868
  1.7 6.4 %collective-permute-start = (bf16[2,1,128,256]{3,2,1,0:T(8,128)(2,1)S(1)}, bf16[2,1,128,256]{3,2,1,0:T(8,128)(2,1)S(1)}, u32[]{:S(2)}, u32[]{:S(2)}) collective-permute-start(bf16[2,1,128,256]{3,2,1,0:T(8,128)(2,1)S(1)} %get-tuple-element.24), channel_id=1, source_target_pairs={{0,1},{1,2},{2,3},{3,4},{4,5},{5,6},{6,7},{7,8},{8,9},{9,10},{10,1... | collective-permute-start | bytes 393224 | tf_op jit(solution)/shard_map/ppermute | solution.py:17
  4.1 5.3 %collective-permute-start.1 = (bf16[2,1,128,256]{3,2,1,0:T(8,128)(2,1)S(1)}, bf16[2,1,128,256]{3,2,1,0:T(8,128)(2,1)S(1)}, u32[]{:S(2)}, u32[]{:S(2)}) collective-permute-start(bf16[2,1,128,256]{3,2,1,0:T(8,128)(2,1)S(1)} %get-tuple-element.25), channel_id=1, source_target_pairs={{1,0},{2,1},{3,2},{4,3},{5,4},{6,5},{7,6},{8,7},{9,8},{10,9},{11,1... | collective-permute-start | bytes 393224 | tf_op jit(solution)/shard_map/ppermute | solution.py:20
  5.4 14.6 %collective-permute-start.3 = (bf16[2,4,128,256]{3,2,1,0:T(8,128)(2,1)}, bf16[2,4,128,256]{3,2,1,0:T(8,128)(2,1)S(1)}, u32[]{:S(2)}, u32[]{:S(2)}) collective-permute-start(bf16[2,4,128,256]{3,2,1,0:T(8,128)(2,1)} %param.7), channel_id=1, source_target_pairs={{16,0},{17,1},{18,2},{19,3},{20,4},{21,5},{22,6},{23,7},{24,8},{25... | collective-permute-start | bytes 1572872 | tf_op jit(solution)/shard_map/ppermute | solution.py:260
  9.6 1.3 %copy-start.2 = (bf16[9,256,256]{2,1,0:T(8,128)(2,1)S(1)}, bf16[9,256,256]{2,1,0:T(8,128)(2,1)}, u32[]{:S(2)}) copy-start(bf16[9,256,256]{2,1,0:T(8,128)(2,1)} %param.5) | copy-start | bytes 3538948
  13.4 6.5 %copy-start = (bf16[2,4,128,256]{3,2,1,0:T(8,128)(2,1)S(1)}, bf16[2,4,128,256]{3,2,1,0:T(8,128)(2,1)}, u32[]{:S(2)}) copy-start(bf16[2,4,128,256]{3,2,1,0:T(8,128)(2,1)} %param.7) | copy-start | bytes 1572868
  13.7 6.3 %copy-start.3 = (bf16[3,256,256]{2,1,0:T(8,128)(2,1)S(1)}, bf16[3,256,256]{2,1,0:T(8,128)(2,1)}, u32[]{:S(2)}) copy-start(bf16[3,256,256]{2,1,0:T(8,128)(2,1)} %param.6) | copy-start | bytes 1179652
  24.3 7.9 %collective-permute-start.4 = (bf16[2,1,128,256]{3,2,1,0:T(8,128)(2,1)S(1)}, bf16[2,1,128,256]{3,2,1,0:T(8,128)(2,1)S(1)}, u32[]{:S(2)}, u32[]{:S(2)}) collective-permute-start(bf16[2,1,128,256]{3,2,1,0:T(8,128)(2,1)S(1)} %get-tuple-element.20), channel_id=1, source_target_pairs={{0,1},{1,2},{2,3},{3,4},{4,5},{5,6},{6,7},{7,8},{8,9},{9,10},{10,1... | collective-permute-start | bytes 393224 | tf_op jit(solution)/shard_map/ppermute | solution.py:17
  28.4 6.8 %collective-permute-start.5 = (bf16[2,1,128,256]{3,2,1,0:T(8,128)(2,1)S(1)}, bf16[2,1,128,256]{3,2,1,0:T(8,128)(2,1)S(1)}, u32[]{:S(2)}, u32[]{:S(2)}) collective-permute-start(bf16[2,1,128,256]{3,2,1,0:T(8,128)(2,1)S(1)} %get-tuple-element.21), channel_id=1, source_target_pairs={{1,0},{2,1},{3,2},{4,3},{5,4},{6,5},{7,6},{8,7},{9,8},{10,9},{11,1... | collective-permute-start | bytes 393224 | tf_op jit(solution)/shard_map/ppermute | solution.py:20
  29.7 10.6 %collective-permute-start.2 = (bf16[2,4,128,256]{3,2,1,0:T(8,128)(2,1)S(1)}, bf16[2,4,128,256]{3,2,1,0:T(8,128)(2,1)S(1)}, u32[]{:S(2)}, u32[]{:S(2)}) collective-permute-start(bf16[2,4,128,256]{3,2,1,0:T(8,128)(2,1)S(1)} %get-tuple-element.5), channel_id=1, source_target_pairs={{0,16},{1,17},{2,18},{3,19},{4,20},{5,21},{6,22},{7,23},{8,24},{9,... | collective-permute-start | bytes 1572872 | tf_op jit(solution)/shard_map/ppermute | solution.py:269

commit v5 on v4

--- a/solution.py
+++ b/solution.py
@@ -112,7 +112,6 @@
     barrier = pltpu.get_barrier_semaphore()
     for bit in orders[0]:
         pl.semaphore_signal(barrier, inc=1, device_id=partner(bit), device_id_type=MESH)
-    pl.semaphore_wait(barrier, stages)
 
     def span(part):
         return pl.ds(part * rows, rows)
@@ -143,7 +142,7 @@
                 sent[part, start + e] = total[at, span(part), :].astype(jnp.bfloat16)
 
         each(count, pack)
-        copy = pltpu.make_async_remote_copy(
+        return pltpu.make_async_remote_copy(
             src_ref=sent.at[part, pl.ds(start, count)],
             dst_ref=landed.at[part, pl.ds(start, count)],
             send_sem=send_sems.at[part, stage],
@@ -151,8 +150,6 @@
             device_id=partner(bit),
             device_id_type=MESH,
         )
-        copy.start()
-        return copy
 
     def add(part, stage):
         free = orders[part][stage + 1 :]
@@ -174,15 +171,22 @@
         each(count, step)
 
     copies = [send(part, 0) for part in range(parts)]
+    pl.semaphore_wait(barrier, stages)
+    for copy in copies:
+        copy.start()
+    started = list(copies)
     for stage in range(stages):
         for part in range(parts):
             copies[part].wait_recv()
             add(part, stage)
-            copies[part].wait_send()
             if stage + 1 < stages:
                 copies[part] = send(part, stage + 1)
+                copies[part].start()
+                started.append(copies[part])
             else:
                 out_ref[span(part), :] = total[fixed(part, stages), span(part), :]
+    for copy in started:
+        copy.wait_send()
 
 
 def exchange(keep, send, axis, step):

time: 73.9 us -> 71.6 us (0.969)
  Pallas kernels: 29.9 us -> 27.6 us
    pallas_call x1, Pallas kernels: 29.9 us -> 27.6 us  [scatter_sums(): pl.pallas_call(functools.partial(scatter_kernel, orders, depth, lanes), o...]
where the time goes in v5:
time: 71.6 us; the launch traced here: 71.3 us
  Pallas kernels  27.6 us (39%)
  matrix products  14.3 us (20%)
  starting transfers between devices  12.2 us (17%)
  waiting for transfers between devices  11 us (15%)
  local copies, waits for them, and re-layouts  4.04 us (6%)
  other arithmetic  1.19 us (2%)
  between operations  1 us (1%)
    pallas_call x1, Pallas kernels, scatter_sums(): pl.pallas_call(functools.partial(scatter_kernel, orders, depth, lanes), o...  27.6 us
    ppermute x2, starting transfers between devices, extended_2(): lax.ppermute(lax.slice_in_dim(block, block.shape[dim] - width, None, axis...  6.44 us
    ppermute x1, waiting for transfers between devices, body(): grad_next = lax.ppermute(grad_out[:2], 'tm', [(t, s) for s, t in onward])  6.19 us
    ppermute x2, waiting for transfers between devices, extended_2(): lax.ppermute(lax.slice_in_dim(block, 0, width, axis=dim), axis, backward)  4.31 us
    dot_general x9, matrix products, body(): lax.dot_general(window, w_space[3 * i + j], (((1,), (1,)), ((), ())), pre...  3.77 us
    dot_general x9, matrix products, body(): lax.dot_general(flat_pre, source, (((0,), (0,)), ((), ())), preferred_ele...  3.02 us
    dot_general x9, matrix products, body(): jnp.dot(window, w_space[3 * i + j], preferred_element_type=jnp.float32)  2.68 us
    ppermute x2, starting transfers between devices, extended_2(): lax.ppermute(lax.slice_in_dim(block, 0, width, axis=dim), axis, backward)  2.58 us
  transfers between devices with their start and end apart: 6, of which 4 were waited for; matrix products, arithmetic and copies ran while one was open for 14% of the time, Pallas kernels for 0%

profile of v5, /device:TPU:0, one launch (start us, length us, event | category | flops | bytes accessed | tf_op | source)
XLA Modules:
  0.0 71.3 jit_solution(11621011689306136796)
XLA Ops:
  0.6 1.0 %fusion.80 = (bf16[2,1,128,256]{3,2,1,0:T(8,128)(2,1)S(1)}, bf16[2,1,128,256]{3,2,1,0:T(8,128)(2,1)S(1)}) fusion(bf16[2,4,128,256]{3,2,1,0:T(8,128)(2,1)} %param.4), kind=kLoop, calls=%fused_computation.123 | loop fusion | bytes 524288 | tf_op jit(solution)/shard_map/slice | solution.py:18
  1.7 2.4 %collective-permute-start = (bf16[2,1,128,256]{3,2,1,0:T(8,128)(2,1)S(1)}, bf16[2,1,128,256]{3,2,1,0:T(8,128)(2,1)S(1)}, u32[]{:S(2)}, u32[]{:S(2)}) collective-permute-start(bf16[2,1,128,256]{3,2,1,0:T(8,128)(2,1)S(1)} %get-tuple-element.24), channel_id=1, source_target_pairs={{0,1},{1,2},{2,3},{3,4},{4,5},{5,6},{6,7},{7,8},{8,9},{9,10},{10,1... | collective-permute-start | bytes 393224 | tf_op jit(solution)/shard_map/ppermute | solution.py:17
  4.1 1.3 %collective-permute-start.1 = (bf16[2,1,128,256]{3,2,1,0:T(8,128)(2,1)S(1)}, bf16[2,1,128,256]{3,2,1,0:T(8,128)(2,1)S(1)}, u32[]{:S(2)}, u32[]{:S(2)}) collective-permute-start(bf16[2,1,128,256]{3,2,1,0:T(8,128)(2,1)S(1)} %get-tuple-element.25), channel_id=1, source_target_pairs={{1,0},{2,1},{3,2},{4,3},{5,4},{6,5},{7,6},{8,7},{9,8},{10,9},{11,1... | collective-permute-start | bytes 393224 | tf_op jit(solution)/shard_map/ppermute | solution.py:20
  5.4 1.3 %collective-permute-start.3 = (bf16[2,4,128,256]{3,2,1,0:T(8,128)(2,1)}, bf16[2,4,128,256]{3,2,1,0:T(8,128)(2,1)S(1)}, u32[]{:S(2)}, u32[]{:S(2)}) collective-permute-start(bf16[2,4,128,256]{3,2,1,0:T(8,128)(2,1)} %param.7), channel_id=1, source_target_pairs={{16,0},{17,1},{18,2},{19,3},{20,4},{21,5},{22,6},{23,7},{24,8},{25... | collective-permute-start | bytes 1572872 | tf_op jit(solution)/shard_map/ppermute | solution.py:264
  6.7 1.4 %fusion.14 = f32[1024,256]{1,0:T(8,128)S(1)} fusion(bf16[1024,256]{1,0:T(8,128)(2,1)} %bitcast.185, bf16[3,256,256]{2,1,0:T(8,128)(2,1)} %param.6), kind=kOutput, calls=%fused_computation.57 | convolution fusion | flops 134217728 | bytes 1703936 | tf_op jit(solution)/shard_map/dot_general | solution.py:50
  8.1 1.3 %collective-permute-done.1 = bf16[2,1,128,256]{3,2,1,0:T(8,128)(2,1)S(1)} collective-permute-done((bf16[2,1,128,256]{3,2,1,0:T(8,128)(2,1)S(1)}, bf16[2,1,128,256]{3,2,1,0:T(8,128)(2,1)S(1)}, u32[]{:S(2)}, u32[]{:S(2)}) %collective-permute-start.1) | collective-permute-done | bytes 131104 | tf_op jit(solution)/shard_map/ppermute | solution.py:20
  9.6 0.4 fusion.78
  10.1 0.8 %copy-done.2 = bf16[9,256,256]{2,1,0:T(8,128)(2,1)S(1)} copy-done((bf16[9,256,256]{2,1,0:T(8,128)(2,1)S(1)}, bf16[9,256,256]{2,1,0:T(8,128)(2,1)}, u32[]{:S(2)}) %copy-start.2) | copy-done | bytes 1179672
  13.7 6.2 %collective-permute-done.3 = bf16[2,4,128,256]{3,2,1,0:T(8,128)(2,1)S(1)} collective-permute-done((bf16[2,4,128,256]{3,2,1,0:T(8,128)(2,1)}, bf16[2,4,128,256]{3,2,1,0:T(8,128)(2,1)S(1)}, u32[]{:S(2)}, u32[]{:S(2)}) %collective-permute-start.3) | collective-permute-done | bytes 524320 | tf_op jit(solution)/shard_map/ppermute | solution.py:264
  20.3 0.4 fusion.6
  20.7 0.5 fusion.12
  21.2 0.3 convolution_bitcast_fusion.3.refs_7_
  21.6 0.3 convolution_bitcast_fusion.9.refs_1_
  21.9 0.3 convolution_bitcast_fusion.4.refs_6_
  22.2 0.3 convolution_bitcast_fusion.5.refs_5_
  22.6 0.3 convolution_bitcast_fusion.6.refs_4_
  23.3 0.3 convolution_bitcast_fusion.8.refs_2_
  23.9 0.3 convolution_bitcast_fusion.2.refs_8_
  24.3 4.1 %collective-permute-start.4 = (bf16[2,1,128,256]{3,2,1,0:T(8,128)(2,1)S(1)}, bf16[2,1,128,256]{3,2,1,0:T(8,128)(2,1)S(1)}, u32[]{:S(2)}, u32[]{:S(2)}) collective-permute-start(bf16[2,1,128,256]{3,2,1,0:T(8,128)(2,1)S(1)} %get-tuple-element.20), channel_id=1, source_target_pairs={{0,1},{1,2},{2,3},{3,4},{4,5},{5,6},{6,7},{7,8},{8,9},{9,10},{10,1... | collective-permute-start | bytes 393224 | tf_op jit(solution)/shard_map/ppermute | solution.py:17
  28.4 1.3 %collective-permute-start.5 = (bf16[2,1,128,256]{3,2,1,0:T(8,128)(2,1)S(1)}, bf16[2,1,128,256]{3,2,1,0:T(8,128)(2,1)S(1)}, u32[]{:S(2)}, u32[]{:S(2)}) collective-permute-start(bf16[2,1,128,256]{3,2,1,0:T(8,128)(2,1)S(1)} %get-tuple-element.21), channel_id=1, source_target_pairs={{1,0},{2,1},{3,2},{4,3},{5,4},{6,5},{7,6},{8,7},{9,8},{10,9},{11,1... | collective-permute-start | bytes 393224 | tf_op jit(solution)/shard_map/ppermute | solution.py:20
  29.7 1.9 %collective-permute-start.2 = (bf16[2,4,128,256]{3,2,1,0:T(8,128)(2,1)S(1)}, bf16[2,4,128,256]{3,2,1,0:T(8,128)(2,1)S(1)}, u32[]{:S(2)}, u32[]{:S(2)}) collective-permute-start(bf16[2,4,128,256]{3,2,1,0:T(8,128)(2,1)S(1)} %get-tuple-element.5), channel_id=1, source_target_pairs={{0,16},{1,17},{2,18},{3,19},{4,20},{5,21},{6,22},{7,23},{8,24},{9,... | collective-permute-start | bytes 1572872 | tf_op jit(solution)/shard_map/ppermute | solution.py:273
  31.9 0.4 convolution_bitcast_fusion.refs_11_
  32.3 3.0 %collective-permute-done.5 = bf16[2,1,128,256]{3,2,1,0:T(8,128)(2,1)S(1)} collective-permute-done((bf16[2,1,128,256]{3,2,1,0:T(8,128)(2,1)S(1)}, bf16[2,1,128,256]{3,2,1,0:T(8,128)(2,1)S(1)}, u32[]{:S(2)}, u32[]{:S(2)}) %collective-permute-start.5) | collective-permute-done | bytes 131104 | tf_op jit(solution)/shard_map/ppermute | solution.py:20
  35.5 0.4 fusion.77
  38.7 1.1 %fusion.7 = bf16[1024,256]{1,0:T(8,128)(2,1)} fusion(f32[1024,256]{1,0:T(8,128)S(1)} %fusion.24, f32[1024,256]{1,0:T(8,128)S(1)} %convolution_add_fusion.1, bf16[1024,256]{1,0:T(8,128)(2,1)S(1)} %bitcast.192, bf16[9,256,256]{2,1,0:T(8,128)(2,1)S(1)} %copy-done.2), kind=kOutput, calls=%fused_computation.25 | convolution fusion | flops 135004160 | bytes 3276800 | tf_op jit(solution)/shard_map/dot_general | solution.py:303
  39.8 0.5 collective-permute-done.2
  40.3 0.3 convolution_bitcast_fusion.1.refs_9_
  40.7 0.3 convolution_bitcast_fusion.11.refs_10_
  41.0 27.6 %shard_map.75 = f32[192,128]{1,0:T(8,128)S(1)} custom-call(f32[256,256]{1,0:T(8,128)S(1)} %convolution_bitcast_fusion.10.refs_0_, f32[256,256]{1,0:T(8,128)S(1)} %convolution_bitcast_fusion.9.refs_1_, f32[256,256]{1,0:T(8,128)S(1)} %convolution_bitcast_fusion.8.refs_2_, f32[256,256]{1,0:T(8,128)S(1)} %convolution_bitcast_fusion.7.refs_3_, ...), custom_call_target="tpu_custom_call" | custom-call | tf_op jit(solution)/shard_map/pallas_call | solution.py:241
  68.6 0.6 slice.195
  69.2 0.6 slice.194
  70.2 1.1 %fusion.5 = bf16[1024,256]{1,0:T(8,128)(2,1)} fusion(f32[1024,256]{1,0:T(8,128)S(1)} %fusion.16, f32[1024,256]{1,0:T(8,128)S(1)} %fusion.20, bf16[1024,256]{1,0:T(8,128)(2,1)S(1)} %bitcast.187, bf16[3,256,256]{2,1,0:T(8,128)(2,1)S(1)} %copy-done.3), kind=kOutput, calls=%fused_computation.23 | convolution fusion | flops 135004160 | bytes 3276800 | tf_op jit(solution)/shard_map/dot_general | solution.py:36
  (38 shorter events, 7.6 us)
Async XLA Ops:
  0.6 8.8 %copy-start.1 = (bf16[2,4,128,256]{3,2,1,0:T(8,128)(2,1)S(1)}, bf16[2,4,128,256]{3,2,1,0:T(8,128)(2,1)}, u32[]{:S(2)}) copy-start(bf16[2,4,128,256]{3,2,1,0:T(8,128)(2,1)} %param.4) | copy-start | bytes 1572868
  1.7 6.4 %collective-permute-start = (bf16[2,1,128,256]{3,2,1,0:T(8,128)(2,1)S(1)}, bf16[2,1,128,256]{3,2,1,0:T(8,128)(2,1)S(1)}, u32[]{:S(2)}, u32[]{:S(2)}) collective-permute-start(bf16[2,1,128,256]{3,2,1,0:T(8,128)(2,1)S(1)} %get-tuple-element.24), channel_id=1, source_target_pairs={{0,1},{1,2},{2,3},{3,4},{4,5},{5,6},{6,7},{7,8},{8,9},{9,10},{10,1... | collective-permute-start | bytes 393224 | tf_op jit(solution)/shard_map/ppermute | solution.py:17
  4.1 5.3 %collective-permute-start.1 = (bf16[2,1,128,256]{3,2,1,0:T(8,128)(2,1)S(1)}, bf16[2,1,128,256]{3,2,1,0:T(8,128)(2,1)S(1)}, u32[]{:S(2)}, u32[]{:S(2)}) collective-permute-start(bf16[2,1,128,256]{3,2,1,0:T(8,128)(2,1)S(1)} %get-tuple-element.25), channel_id=1, source_target_pairs={{1,0},{2,1},{3,2},{4,3},{5,4},{6,5},{7,6},{8,7},{9,8},{10,9},{11,1... | collective-permute-start | bytes 393224 | tf_op jit(solution)/shard_map/ppermute | solution.py:20
  5.4 14.6 %collective-permute-start.3 = (bf16[2,4,128,256]{3,2,1,0:T(8,128)(2,1)}, bf16[2,4,128,256]{3,2,1,0:T(8,128)(2,1)S(1)}, u32[]{:S(2)}, u32[]{:S(2)}) collective-permute-start(bf16[2,4,128,256]{3,2,1,0:T(8,128)(2,1)} %param.7), channel_id=1, source_target_pairs={{16,0},{17,1},{18,2},{19,3},{20,4},{21,5},{22,6},{23,7},{24,8},{25... | collective-permute-start | bytes 1572872 | tf_op jit(solution)/shard_map/ppermute | solution.py:264
  9.6 1.3 %copy-start.2 = (bf16[9,256,256]{2,1,0:T(8,128)(2,1)S(1)}, bf16[9,256,256]{2,1,0:T(8,128)(2,1)}, u32[]{:S(2)}) copy-start(bf16[9,256,256]{2,1,0:T(8,128)(2,1)} %param.5) | copy-start | bytes 3538948
  13.4 6.5 %copy-start = (bf16[2,4,128,256]{3,2,1,0:T(8,128)(2,1)S(1)}, bf16[2,4,128,256]{3,2,1,0:T(8,128)(2,1)}, u32[]{:S(2)}) copy-start(bf16[2,4,128,256]{3,2,1,0:T(8,128)(2,1)} %param.7) | copy-start | bytes 1572868
  13.7 6.3 %copy-start.3 = (bf16[3,256,256]{2,1,0:T(8,128)(2,1)S(1)}, bf16[3,256,256]{2,1,0:T(8,128)(2,1)}, u32[]{:S(2)}) copy-start(bf16[3,256,256]{2,1,0:T(8,128)(2,1)} %param.6) | copy-start | bytes 1179652
  24.3 7.9 %collective-permute-start.4 = (bf16[2,1,128,256]{3,2,1,0:T(8,128)(2,1)S(1)}, bf16[2,1,128,256]{3,2,1,0:T(8,128)(2,1)S(1)}, u32[]{:S(2)}, u32[]{:S(2)}) collective-permute-start(bf16[2,1,128,256]{3,2,1,0:T(8,128)(2,1)S(1)} %get-tuple-element.20), channel_id=1, source_target_pairs={{0,1},{1,2},{2,3},{3,4},{4,5},{5,6},{6,7},{7,8},{8,9},{9,10},{10,1... | collective-permute-start | bytes 393224 | tf_op jit(solution)/shard_map/ppermute | solution.py:17
  28.4 6.8 %collective-permute-start.5 = (bf16[2,1,128,256]{3,2,1,0:T(8,128)(2,1)S(1)}, bf16[2,1,128,256]{3,2,1,0:T(8,128)(2,1)S(1)}, u32[]{:S(2)}, u32[]{:S(2)}) collective-permute-start(bf16[2,1,128,256]{3,2,1,0:T(8,128)(2,1)S(1)} %get-tuple-element.21), channel_id=1, source_target_pairs={{1,0},{2,1},{3,2},{4,3},{5,4},{6,5},{7,6},{8,7},{9,8},{10,9},{11,1... | collective-permute-start | bytes 393224 | tf_op jit(solution)/shard_map/ppermute | solution.py:20
  29.7 10.6 %collective-permute-start.2 = (bf16[2,4,128,256]{3,2,1,0:T(8,128)(2,1)S(1)}, bf16[2,4,128,256]{3,2,1,0:T(8,128)(2,1)S(1)}, u32[]{:S(2)}, u32[]{:S(2)}) collective-permute-start(bf16[2,4,128,256]{3,2,1,0:T(8,128)(2,1)S(1)} %get-tuple-element.5), channel_id=1, source_target_pairs={{0,16},{1,17},{2,18},{3,19},{4,20},{5,21},{6,22},{7,23},{8,24},{9,... | collective-permute-start | bytes 1572872 | tf_op jit(solution)/shard_map/ppermute | solution.py:273
